TPU v7x, 128 devices: a whole 4x4x4 slice. The times are simulated.
128 devices in a mesh: slab: 32 (over x, z, core), cable: 4 (over y).
Axes of the slice: x: 4, y: 4, z: 4, core: 2. Of those that a mesh axis runs over, the one named last changes fastest.
Arguments:
- electric: float32 [3, 1024, 128, 256], P(None, ('slab', 'cable')), may hold values from -6 to 6
- magnetic: float32 [3, 1024, 128, 256], P(None, ('slab', 'cable')), may hold values from -6 to 6
- conductivity: float32 [1024, 128, 256], P(('slab', 'cable')), may hold values from 0.02 to 0.8
- voltage: float32 [32, 128, 16384], P(None, None, ('slab', 'cable')), may hold values from -6 to 6
- current: float32 [32, 128, 16384], P(None, None, ('slab', 'cable')), may hold values from -6 to 6
- inverse_inductance: float32 [32, 32, 16384], P(None, None, ('slab', 'cable')), as said below
- inverse_capacitance: float32 [32, 32, 16384], P(None, None, ('slab', 'cable')), as said below
- tangent: float32 [3, 128, 16384], P(None, ('slab', 'cable')), may hold values from -4 to 4
- sample_cell: int32 [128, 16384], P(('slab', 'cable')), may hold values from 0 to 1023
- tube_length: int32 [16384], P(('slab', 'cable')), may hold values from 32 to 128
- junction_link: int32 [16384], P(('slab', 'cable')), may hold values from 0 to 127, as said below
Outputs:
- electric_new: float32 [3, 1024, 128, 256], P(None, ('slab', 'cable'))
- magnetic_new: float32 [3, 1024, 128, 256], P(None, ('slab', 'cable'))
- voltage_new: float32 [32, 128, 16384], P(None, None, ('slab', 'cable'))
- current_new: float32 [32, 128, 16384], P(None, None, ('slab', 'cable'))
Inputs may be any that keep to these rules, and one draw needn't show every extreme that they name: `junction_link`: every aligned block of 128 entries holds each of its values once. `inverse_inductance`: symmetric, with off-diagonal entries summing to about as much as the diagonal. `inverse_capacitance`: symmetric, with off-diagonal entries summing to about as much as the diagonal.
All inputs are finite; a program needn't handle non-finite values.
Results may differ from a plain program's by a relative error of at most 0.0001.
Values sent between devices are 32-bit elements; how exact they have to be, the bound alone decides.
No kernel may reach another device: no remote copies, remote signals or barrier semaphores. Data moves between devices by JAX's collectives and lax.ppermute only.
A program may use at most 128 MiB of HBM per device.

v0:
```python
import jax
import jax.numpy as jnp
from jax import lax
from jax.experimental import pallas as pl
from jax.experimental.pallas import tpu as pltpu
from jax.sharding import PartitionSpec as P

F = jnp.float32
B16 = jnp.bfloat16
I32 = jnp.int32
SUB = 3
COURANT = 0.5
MB = 2**20


def take(x, index, axis):
    return jnp.take_along_axis(x, index, axis=axis, mode="promise_in_bounds")


def iota(shape, axis):
    return lax.broadcasted_iota(I32, shape, axis)


def call(body, out, *ins, name, scratch=(), limit=40, in_specs=None, aliases=None, out_specs=None, cost=None, grid=()):
    kw = {}
    if in_specs is not None:
        kw["in_specs"] = in_specs
    if out_specs is not None:
        kw["out_specs"] = out_specs
    return pl.pallas_call(
        body,
        out_shape=out,
        grid=grid,
        scratch_shapes=list(scratch),
        input_output_aliases=aliases or {},
        compiler_params=pltpu.CompilerParams(vmem_limit_bytes=limit * MB),
        cost_estimate=cost,
        name=name,
        **kw,
    )(*ins)


def shape(*dims, dtype=F):
    return jax.ShapeDtypeStruct(dims, dtype)


def gather_kernel(e_ref, idx_ref, tan_ref, drive_ref, layer_ref):
    layer_ref[...] = e_ref[1:3, 0]
    for h in range(2):
        lanes = pl.ds(h * 128, 128)
        rows = pl.ds(h, 64, stride=2)
        idx = idx_ref[rows, :]
        idx = [idx[8 * g : 8 * g + 8] for g in range(8)]
        low = [i & 7 for i in idx]
        high = [i >> 3 for i in idx]

        def step(b, acc):
            acc = list(acc)
            x = b // 16
            yrows = pl.ds(pl.multiple_of((b % 16) * 8, 8), 8)
            src = [e_ref[k, x, yrows, lanes] for k in range(3)]
            for g in range(8):
                hit = high[g] == b
                for k in range(3):
                    acc[g * 3 + k] = jnp.where(hit, take(src[k], low[g], 0), acc[g * 3 + k])
            return tuple(acc)

        acc = lax.fori_loop(0, 128, step, (jnp.zeros((8, 128), F),) * 24, unroll=4)
        picked = [jnp.concatenate([acc[g * 3 + k] for g in range(8)], 0) for k in range(3)]
        steer = [tan_ref[k, rows, :] for k in range(3)]
        drive_ref[rows, :] = steer[0] * picked[0] + steer[1] * picked[1] + steer[2] * picked[2]


def merge_pair(x, y):
    low = iota((8, 128), 0) < 4
    return jnp.where(low, x, pltpu.roll(y, 4, 0)), jnp.where(low, pltpu.roll(x, 4, 0), y)


def split_parts(x):
    high = x.astype(B16)
    return high, (x - high.astype(F)).astype(B16)


def line_kernel(
    v_ref, i_ref, a_ref, b_ref, drive_ref, len_ref,
    vo_ref, io_ref, ends_ref, ind_ref,
    vt, it, at, vg, ig, ah, bh, dg, eg, indt,
):
    sub8 = iota((8, 128), 0)
    lane8 = iota((8, 128), 1)
    lane = iota((128, 128), 1)

    def turn_in(c, carry):
        vt[c] = v_ref[c].T
        it[c] = i_ref[c].T
        return carry

    lax.fori_loop(0, 32, turn_in, 0, unroll=4)

    spread = [(sub8 >> 2) + 2 * j for j in range(4)]
    own = (sub8 & 3) == (lane8 & 3)
    for m_ref, dst in ((a_ref, ah), (b_ref, bh)):

        def expand(c, carry):
            tiles = []
            for q in range(4):
                tile = m_ref[c, 8 * q : 8 * q + 8, :]
                for j in range(4):
                    tiles.append(jnp.where(own, take(tile, spread[j], 0), 0.0))
            at[c] = jnp.concatenate(tiles, 0).T
            return carry

        lax.fori_loop(0, 32, expand, 0, unroll=4)

        def pack(b, carry):
            rows = pl.ds(pl.multiple_of(b * 8, 8), 8)
            first, second = [], []
            for i in range(16):
                g0, g1 = merge_pair(at[2 * i, rows, :], at[2 * i + 1, rows, :])
                first.append(g0)
                second.append(g1)
            for p, tiles in enumerate((first, second)):
                high, low = split_parts(jnp.concatenate(tiles, 0))
                out_rows = pl.ds(pl.multiple_of(b * 256 + p * 128, 128), 128)
                dst[out_rows, 0:128] = high
                dst[out_rows, 128:256] = low
            return carry

        lax.fori_loop(0, 16, pack, 0, unroll=2)

    drive_t = drive_ref[...].T
    at[0] = drive_t
    at[1] = jnp.broadcast_to(len_ref[...].astype(F), (128, 128)).T
    for b in range(16):
        rows = slice(8 * b, 8 * b + 8)
        for p, value in enumerate(merge_pair(at[0, rows, :], at[0, rows, :])):
            dg[16 * b + 8 * p : 16 * b + 8 * p + 8, :] = value
        for p, value in enumerate(merge_pair(at[1, rows, :], at[1, rows, :])):
            eg[16 * b + 8 * p : 16 * b + 8 * p + 8, :] = value.astype(I32)

    def regroup(b, carry):
        rows = pl.ds(pl.multiple_of(b * 8, 8), 8)
        for src, dst in ((vt, vg), (it, ig)):
            for i in range(16):
                g0, g1 = merge_pair(src[2 * i, rows, :], src[2 * i + 1, rows, :])
                dst[pl.ds(pl.multiple_of(b * 256 + 8 * i, 8), 8), :] = g0
                dst[pl.ds(pl.multiple_of(b * 256 + 128 + 8 * i, 8), 8), :] = g1
        return carry

    lax.fori_loop(0, 16, regroup, 0, unroll=2)

    def product(m_ref, rows, x):
        high, low = split_parts(x)
        rhs = jnp.concatenate([high, low], 1)
        rhs = jnp.concatenate([rhs, rhs], 0)
        y = jnp.dot(m_ref[rows, :], rhs, preferred_element_type=F)
        return y[:, :128] + y[:, 128:]

    unroll = 16
    for substep in range(SUB):

        def current_step(n, acc):
            for u in range(unroll):
                g = n * unroll + u
                rows = pl.ds(pl.multiple_of(g * 128, 128), 128)
                small = pl.ds(pl.multiple_of(g * 8, 8), 8)
                length = eg[small, :]
                live = jnp.concatenate([lane8 < length] * 16, 0)
                drive = jnp.concatenate([dg[small, :]] * 16, 0)
                volts = vg[rows, :]
                ahead = jnp.where(lane == 127, 0.0, pltpu.roll(volts, 127, 1))
                y = product(ah, rows, ahead - volts - drive)
                amps = jnp.where(live, ig[rows, :] - y, 0.0)
                ig[rows, :] = amps
                spot = lane8 == 4 * g + (sub8 & 3)
                acc = tuple(
                    jnp.where(spot, take(amps[8 * i : 8 * i + 8], length - 1, 1), acc[i])
                    for i in range(16)
                )
            return acc

        acc = lax.fori_loop(0, 32 // unroll, current_step, (jnp.zeros((8, 128), F),) * 16)
        pick = (sub8 & 1) * 4 + (lane8 & 3)
        for q in range(4):
            out = take(acc[4 * q], pick, 0)
            for i in range(1, 4):
                out = jnp.where((sub8 >> 1) == i, take(acc[4 * q + i], pick, 0), out)
            ends_ref[substep, 8 * q : 8 * q + 8, :] = out

        def voltage_step(n, carry):
            for u in range(unroll):
                g = n * unroll + u
                rows = pl.ds(pl.multiple_of(g * 128, 128), 128)
                small = pl.ds(pl.multiple_of(g * 8, 8), 8)
                live = jnp.concatenate([lane8 < eg[small, :]] * 16, 0)
                amps = ig[rows, :]
                behind = jnp.where(lane == 0, 0.0, pltpu.roll(amps, 1, 1))
                y = product(bh, rows, amps - behind)
                vg[rows, :] = jnp.where(live, vg[rows, :] - y, 0.0)
            return carry

        lax.fori_loop(0, 32 // unroll, voltage_step, 0)

    def ungroup(b, carry):
        rows = pl.ds(pl.multiple_of(b * 8, 8), 8)
        for src, dst in ((vg, vt), (ig, it)):
            sums = [None, None]
            for i in range(16):
                g0 = src[pl.ds(pl.multiple_of(b * 256 + 8 * i, 8), 8), :]
                g1 = src[pl.ds(pl.multiple_of(b * 256 + 128 + 8 * i, 8), 8), :]
                c0, c1 = merge_pair(g0, g1)
                dst[2 * i, rows, :] = c0
                dst[2 * i + 1, rows, :] = c1
                if src is ig:
                    sums = [c0 + c1 if s is None else s + c0 + c1 for s in sums[:1]] + [None]
            if src is ig:
                indt[rows, :] = sums[0] * (1.0 / 32.0)
        return carry

    lax.fori_loop(0, 16, ungroup, 0, unroll=2)

    def turn_out(c, carry):
        vo_ref[c] = vt[c].T
        io_ref[c] = it[c].T
        return carry

    lax.fori_loop(0, 32, turn_out, 0, unroll=4)
    ind_ref[...] = indt[...].T


def lines(voltage, current, inductance, capacitance, drive, lengths):
    big = pltpu.VMEM((32, 128, 128), F)
    flat = pltpu.VMEM((4096, 128), F)
    packed = pltpu.VMEM((4096, 256), B16)
    return call(
        line_kernel,
        (shape(32, 128, 128), shape(32, 128, 128), shape(3, 32, 128), shape(128, 128)),
        voltage, current, inductance, capacitance, drive, lengths,
        name="lines",
        scratch=[big, big, big, flat, flat, packed, packed,
                 pltpu.VMEM((256, 128), F), pltpu.VMEM((256, 128), I32), pltpu.VMEM((128, 128), F)],
        limit=40,
    )


def junction_kernel(ends_ref, link_ref, a_ref, b_ref, v_ref, i_ref, ind_ref, vo_ref, io_ref, indo_ref, buf):
    link = jnp.broadcast_to(link_ref[...], (8, 128))
    inflow = [
        jnp.concatenate([take(ends_ref[k, 8 * q : 8 * q + 8, :], link, 1) for q in range(4)], 0)
        for k in range(SUB)
    ]

    def apply(m_ref, x):
        buf[...] = x
        parts = [None] * 4
        for d in range(32):
            term = m_ref[d] * buf[d : d + 1, :]
            parts[d % 4] = term if parts[d % 4] is None else parts[d % 4] + term
        return (parts[0] + parts[1]) + (parts[2] + parts[3])

    f1, f2, f3 = inflow
    v1 = apply(b_ref, f1)
    i2 = apply(a_ref, v1)
    v2b = apply(b_ref, i2)
    v2a = v1 - v2b + apply(b_ref, f2)
    i3a = i2 - apply(a_ref, v2b - v2a)
    i3b = apply(a_ref, v2b)
    v3c = apply(b_ref, i3b)
    v3a = v2a - apply(b_ref, i3a - f3)
    v3b = v2b - v3c + apply(b_ref, i3a)
    sub8 = iota((8, 128), 0)
    for c in range(32):
        row = slice(c, c + 1)
        add = jnp.where(sub8 == 0, v3a[row], jnp.where(sub8 == 1, v3b[row], jnp.where(sub8 == 2, v3c[row], 0.0)))
        vo_ref[c] = v_ref[c] + add
        add = jnp.where(sub8 == 0, i3a[row], jnp.where(sub8 == 1, i3b[row], 0.0))
        io_ref[c] = i_ref[c] + add
    mean_a = jnp.sum(i3a, axis=0, keepdims=True) * (1.0 / 32.0)
    mean_b = jnp.sum(i3b, axis=0, keepdims=True) * (1.0 / 32.0)
    indo_ref[...] = ind_ref[...]
    indo_ref[0:8, :] = ind_ref[0:8, :] + jnp.where(sub8 == 0, mean_a, jnp.where(sub8 == 1, mean_b, 0.0))


def junctions(ends, link, inductance, capacitance, volts, amps, induced):
    head = pl.BlockSpec((32, 8, 128), lambda n: (0, 0, 0))
    whole = lambda *dims: pl.BlockSpec(dims, lambda n: (0,) * len(dims))
    return call(
        junction_kernel,
        (shape(32, 128, 128), shape(32, 128, 128), shape(128, 128)),
        ends, link, inductance, capacitance, volts, amps, induced,
        name="junctions",
        grid=(1,),
        in_specs=[whole(3, 32, 128), whole(1, 128), whole(32, 32, 128), whole(32, 32, 128), head, head, whole(128, 128)],
        out_specs=(head, head, whole(128, 128)),
        aliases={4: 0, 5: 1},
        scratch=[pltpu.VMEM((32, 128), F)],
        limit=16,
    )


def magnetic_kernel(e_ref, h_ref, above_ref, ho_ref, layer_ref):
    sub = iota((8, 256), 0)
    lane = iota((8, 256), 1)

    def one_layer(x, carry):
        nx = jnp.minimum(x + 1, 7)
        last = x == 7
        for yb in range(16):
            rows = slice(8 * yb, 8 * yb + 8)
            e = [e_ref[k, x, rows, :] for k in range(3)]
            ahead = [jnp.where(last, above_ref[k, rows, :], e_ref[k + 1, nx, rows, :]) for k in range(2)]

            def diff_y(k):
                rolled = pltpu.roll(e[k], 7, 0)
                edge = e_ref[k, x, 8 * yb + 8 : 8 * yb + 9, :] if yb < 15 else jnp.zeros((1, 256), F)
                return jnp.where(sub == 7, edge, rolled) - e[k]

            def diff_z(k):
                return jnp.where(lane == 255, 0.0, pltpu.roll(e[k], 255, 1)) - e[k]

            curl = (
                diff_y(2) - diff_z(1),
                diff_z(0) - (ahead[1] - e[2]),
                (ahead[0] - e[1]) - diff_y(0),
            )
            for k in range(3):
                ho_ref[k, x, rows, :] = h_ref[k, x, rows, :] - COURANT * curl[k]
        return carry

    lax.fori_loop(0, 8, one_layer, 0)
    layer_ref[...] = ho_ref[1:3, 7]


def magnetics(electric, magnetic, above):
    return call(
        magnetic_kernel,
        (shape(3, 8, 128, 256), shape(2, 128, 256)),
        electric, magnetic, above,
        name="magnetics",
        limit=24,
    )


def sort_columns(keys):
    sub8 = iota((8, 128), 0)
    keys = list(keys)
    size = 2
    while size <= 128:
        stride = size // 2
        while stride >= 1:
            if stride >= 8:
                gap = stride // 8
                for n in range(16):
                    if n & gap:
                        continue
                    rising = ((n * 8) & size) == 0 or size == 128
                    low = jnp.minimum(keys[n], keys[n + gap])
                    high = jnp.maximum(keys[n], keys[n + gap])
                    keys[n], keys[n + gap] = (low, high) if rising else (high, low)
            else:
                partner = sub8 ^ stride
                first = (sub8 & stride) == 0
                for n in range(16):
                    other = take(keys[n], partner, 0)
                    if size >= 8:
                        rising = ((n * 8) & size) == 0 or size == 128
                        want_low = first if rising else ~first
                    else:
                        want_low = ((sub8 & size) == 0) == first
                    keys[n] = jnp.where(want_low, jnp.minimum(keys[n], other), jnp.maximum(keys[n], other))
            stride //= 2
        size *= 2
    return keys


def electric_kernel(
    e_ref, h_ref, below_ref, sigma_ref, ind_ref, tan_ref, idx_ref,
    eo_ref, cell_s, perm_s, val_s, dep_s, plane_s,
):
    sub8 = iota((8, 128), 0)
    lane8 = iota((8, 128), 1)
    keys = []
    for n in range(16):
        owner = sub8 + 8 * n
        cell = idx_ref[8 * n : 8 * n + 8, :]
        keys.append(((owner & 1) * 1024 + cell) * 128 + owner)
    keys = jnp.concatenate(sort_columns(keys), 0).T
    cell_s[...] = keys >> 7
    perm_s[...] = keys & 127

    for k in range(3):
        val_s[k] = (tan_ref[k] * ind_ref[...]).T
    for n in range(16):
        rows = slice(8 * n, 8 * n + 8)
        perm = perm_s[rows, :]
        cell = cell_s[rows, :]
        val = [take(val_s[k, rows, :], perm, 1) for k in range(3)]
        for gap in (1, 2, 4, 8, 16, 32):
            same = pltpu.roll(cell, gap, 1) == cell
            val = [v + jnp.where(same, pltpu.roll(v, gap, 1), 0.0) for v in val]
        for k in range(3):
            val_s[k, rows, :] = val[k]

    def spread(n, carry):
        rows = pl.ds(pl.multiple_of(n * 8, 8), 8)
        cell = cell_s[rows, :]
        val = [val_s[k, rows, :] for k in range(3)]
        for h in range(2):
            fence = {
                p: take(cell, jnp.full((8, 128), 64 * h + p, I32), 1)
                for p in (0, 8, 16, 24, 32, 40, 48, 56)
            }
            for x in range(8):
                target = lane8 + (h * 1024 + x * 128)
                up = fence[32] <= target
                pos = jnp.where(up, 64 * h + 32, 64 * h)
                cur = jnp.where(up, fence[32], fence[0])
                probe = jnp.where(up, fence[48], fence[16])
                up2 = probe <= target
                pos = jnp.where(up2, pos + 16, pos)
                cur = jnp.where(up2, probe, cur)
                probe = jnp.where(
                    up,
                    jnp.where(up2, fence[56], fence[40]),
                    jnp.where(up2, fence[24], fence[8]),
                )
                hit = probe <= target
                pos = jnp.where(hit, pos + 8, pos)
                cur = jnp.where(hit, probe, cur)
                for step in (4, 2, 1):
                    probe = take(cell, pos + step, 1)
                    hit = probe <= target
                    pos = jnp.where(hit, pos + step, pos)
                    cur = jnp.where(hit, probe, cur)
                found = cur == target
                for k in range(3):
                    dep_s[h, k, x, rows, :] = jnp.where(found, take(val[k], pos, 1), 0.0)
        return carry

    lax.fori_loop(0, 16, spread, 0)

    sub = iota((8, 256), 0)
    lane = iota((8, 256), 1)

    def one_layer(x, carry):
        px = jnp.maximum(x - 1, 0)
        first = x == 0
        for k in range(3):
            for h in range(2):
                plane_s[k, :, 128 * h : 128 * h + 128] = dep_s[h, k, x].T
        for yb in range(16):
            rows = slice(8 * yb, 8 * yb + 8)
            m = [h_ref[k, x, rows, :] for k in range(3)]
            behind = [jnp.where(first, below_ref[k, rows, :], h_ref[k + 1, px, rows, :]) for k in range(2)]

            def diff_y(k):
                rolled = pltpu.roll(m[k], 1, 0)
                edge = h_ref[k, x, 8 * yb - 1 : 8 * yb, :] if yb > 0 else jnp.zeros((1, 256), F)
                return m[k] - jnp.where(sub == 0, edge, rolled)

            def diff_z(k):
                return m[k] - jnp.where(lane == 0, 0.0, pltpu.roll(m[k], 1, 1))

            curl = (
                diff_y(2) - diff_z(1),
                diff_z(0) - (m[2] - behind[1]),
                (m[1] - behind[0]) - diff_y(0),
            )
            sigma = sigma_ref[x, rows, :]
            inverse = 1.0 / (1.0 + sigma)
            keep = (1.0 - sigma) * inverse
            push = COURANT * inverse
            for k in range(3):
                eo_ref[k, x, rows, :] = keep * e_ref[k, x, rows, :] + push * (curl[k] - plane_s[k, rows, :])
        return carry

    lax.fori_loop(0, 8, one_layer, 0)


def electrics(electric, magnetic_new, below, conductivity, induced, tangent, cells):
    return call(
        electric_kernel,
        shape(3, 8, 128, 256),
        electric, magnetic_new, below, conductivity, induced, tangent, cells,
        name="electrics",
        scratch=[
            pltpu.VMEM((128, 128), I32),
            pltpu.VMEM((128, 128), I32),
            pltpu.VMEM((3, 128, 128), F),
            pltpu.VMEM((2, 3, 8, 128, 128), F),
            pltpu.VMEM((3, 128, 256), F),
        ],
        limit=30,
    )


BOTH = ("slab", "cable")


def along(x, axis, by):
    peers = lax.axis_size(axis)
    return lax.ppermute(x, axis, [(i, i + by) for i in range(peers) if 0 <= i + by < peers])


def around(x, axis):
    peers = lax.axis_size(axis)
    return lax.ppermute(x, axis, [(i, (i + 1) % peers) for i in range(peers)])


def exchange(x):
    return lax.all_to_all(x, BOTH, split_axis=0, concat_axis=0, tiled=True)


def local(
    electric, magnetic, conductivity, voltage, current, inverse_inductance,
    inverse_capacitance, tangent, sample_cell, tube_length, junction_link,
):
    cells = sample_cell.reshape(128, 128)
    steer = tangent.reshape(3, 128, 128)
    drive_local, layer = call(
        gather_kernel, (shape(128, 128), shape(2, 128, 256)), electric, cells, steer, name="gather", limit=20
    )
    above = along(layer, BOTH, -1)
    drive = exchange(drive_local)
    volts, amps, ends, induced = lines(
        voltage, current, inverse_inductance, inverse_capacitance, drive, tube_length.reshape(1, 128)
    )
    ends = around(ends, "cable")
    magnetic_new, layer = magnetics(electric, magnetic, above)
    below = along(layer, BOTH, 1)
    volts, amps, induced = junctions(
        ends, junction_link.reshape(1, 128), inverse_inductance, inverse_capacitance, volts, amps, induced
    )
    induced_local = exchange(induced)
    electric_new = electrics(electric, magnetic_new, below, conductivity, induced_local, steer, cells)
    return electric_new, magnetic_new, volts, amps


def solution(mesh):
    grid = P(None, BOTH, None, None)
    tubes = P(None, None, BOTH)
    return jax.shard_map(
        local,
        mesh=mesh,
        in_specs=(
            grid, grid, P(BOTH, None, None), tubes, tubes, tubes, tubes,
            P(None, BOTH, None), P(BOTH, None), P(BOTH), P(BOTH),
        ),
        out_specs=(grid, grid, tubes, tubes),
        check_vma=False,
    )
```

profile of v0, /device:TPU:1, one launch (start us, length us, event | category | flops | bytes accessed | tf_op | source)
XLA Modules:
  0.0 101.0 jit_solution(8479542624541092265)
XLA Ops:
  0.6 0.0 copy-start
  0.6 1.9 %copy-done = f32[3,8,128,256]{3,2,1,0:T(8,128)S(1)} copy-done((f32[3,8,128,256]{3,2,1,0:T(8,128)S(1)}, f32[3,8,128,256]{3,2,1,0:T(8,128)}, u32[]{:S(2)}) %copy-start) | copy-done | bytes 3145752
  2.5 0.9 copy-done.9
  3.5 0.8 copy-done.11
  4.3 2.8 %gather.1 = (f32[128,128]{1,0:T(8,128)S(1)}, f32[2,128,256]{2,1,0:T(8,128)S(1)}) custom-call(f32[3,8,128,256]{3,2,1,0:T(8,128)S(1)} %copy-done, s32[128,128]{1,0:T(8,128)S(1)} %bitcast.16, f32[3,128,128]{2,1,0:T(8,128)S(1)} %bitcast.12), custom_call_target="tpu_custom_call" | custom-call | tf_op jit(solution)/shard_map/gather/pallas_call | solution.py:30
  7.1 0.0 copy-start.13
  7.1 6.0 %collective-permute-start = (f32[2,128,256]{2,1,0:T(8,128)S(1)}, f32[2,128,256]{2,1,0:T(8,128)S(1)}, u32[]{:S(2)}, u32[]{:S(2)}) collective-permute-start(f32[2,128,256]{2,1,0:T(8,128)S(1)} %get-tuple-element.15), channel_id=1, source_target_pairs={{1,0},{2,1},{3,2},{4,3},{5,4},{6,5},{7,6},{8,7},{9,8},{10,9},{11,1... | collective-permute-start | bytes 786440 | tf_op jit(solution)/shard_map/ppermute | solution.py:502
  13.2 3.6 %collective-permute-done.above_ref = f32[2,128,256]{2,1,0:T(8,128)S(1)} collective-permute-done((f32[2,128,256]{2,1,0:T(8,128)S(1)}, f32[2,128,256]{2,1,0:T(8,128)S(1)}, u32[]{:S(2)}, u32[]{:S(2)}) %collective-permute-start) | collective-permute-done | bytes 262176 | tf_op jit(solution)/shard_map/ppermute | solution.py:502
  16.8 0.0 copy-done.1
  16.8 1.9 %copy-done.2 = f32[3,8,128,256]{3,2,1,0:T(8,128)S(1)} copy-done((f32[3,8,128,256]{3,2,1,0:T(8,128)S(1)}, f32[3,8,128,256]{3,2,1,0:T(8,128)}, u32[]{:S(2)}) %copy-start.2) | copy-done | bytes 3145752
  18.7 3.0 %magnetics.1 = (f32[3,8,128,256]{3,2,1,0:T(8,128)}, f32[2,128,256]{2,1,0:T(8,128)S(1)}) custom-call(f32[3,8,128,256]{3,2,1,0:T(8,128)S(1)} %copy-done.1, f32[3,8,128,256]{3,2,1,0:T(8,128)S(1)} %copy-done.2, f32[2,128,256]{2,1,0:T(8,128)S(1)} %collective-permute-done.above_ref), custom_call_target="tpu_custom_call" | custom-call | tf_op jit(solution)/shard_map/magnetics/pallas_call | solution.py:30
  21.7 3.4 %collective-permute-start.1 = (f32[2,128,256]{2,1,0:T(8,128)S(1)}, f32[2,128,256]{2,1,0:T(8,128)S(1)}, u32[]{:S(2)}, u32[]{:S(2)}) collective-permute-start(f32[2,128,256]{2,1,0:T(8,128)S(1)} %get-tuple-element.17), channel_id=1, source_target_pairs={{0,1},{1,2},{2,3},{3,4},{4,5},{5,6},{6,7},{7,8},{8,9},{9,10},{10,1... | collective-permute-start | bytes 786440 | tf_op jit(solution)/shard_map/ppermute | solution.py:502
  25.2 22.8 %all_to_all.22 = f32[128,1,128]{2,1,0:T(1,128)S(1)} all-to-all(f32[128,1,128]{2,1,0:T(1,128)S(1)} %bitcast.18), channel_id=1, replica_groups=mesh['slab'=32,'cable'=4] {'slab','cable'}, dimensions={0} | all-to-all | bytes 131072 | tf_op jit(solution)/shard_map/all_to_all | solution.py:511
  48.0 0.0 copy-done.13
  48.0 0.0 copy-done.4
  48.0 0.0 copy-done.5
  48.0 0.0 copy-done.6
  48.0 0.0 copy-done.7
  48.0 0.0 copy-start.14
  48.0 19.1 %lines.1 = (f32[32,128,128]{2,1,0:T(8,128)}, f32[32,128,128]{2,1,0:T(8,128)}, f32[3,32,128]{2,1,0:T(8,128)S(1)}, f32[128,128]{1,0:T(8,128)S(1)}) custom-call(f32[32,128,128]{2,1,0:T(8,128)S(1)} %copy-done.4, f32[32,128,128]{2,1,0:T(8,128)S(1)} %copy-done.5, f32[32,32,128]{2,1,0:T(8,128)S(1)} %copy-done.6, f32[32,32,128]{2,1,0:T(8,128)S(1)} %copy-done.7, ...), custom_call_target="tpu_custom_call" | custom-call | tf_op jit(solution)/shard_map/lines/pallas_call | solution.py:30
  67.2 0.3 collective-permute-start.2
  67.5 3.8 %collective-permute-done.2.ends_ref = f32[3,32,128]{2,1,0:T(8,128)S(1)} collective-permute-done((f32[3,32,128]{2,1,0:T(8,128)S(1)}, f32[3,32,128]{2,1,0:T(8,128)S(1)}, u32[]{:S(2)}, u32[]{:S(2)}) %collective-permute-start.2) | collective-permute-done | bytes 49184 | tf_op jit(solution)/shard_map/ppermute | solution.py:507
  71.3 0.0 copy-done.14
  71.3 0.0 copy-start.12
  71.3 2.3 %junctions.1 = (f32[32,128,128]{2,1,0:T(8,128)}, f32[32,128,128]{2,1,0:T(8,128)}, f32[128,128]{1,0:T(8,128)S(1)}) custom-call(f32[3,32,128]{2,1,0:T(8,128)S(1)} %collective-permute-done.2.ends_ref, s32[1,128]{1,0:T(1,128)S(1)} %bitcast.21, f32[32,32,128]{2,1,0:T(8,128)S(1)} %copy-done.6, ...), custom_call_target="tpu_custom_call", output_to_operand_aliasing={{0}: (4, {}), {1}: (5, {})} | custom-call | tf_op jit(solution)/shard_map/junctions/pallas_call | solution.py:30
  73.6 14.4 %all_to_all.23 = f32[128,1,128]{2,1,0:T(1,128)S(1)} all-to-all(f32[128,1,128]{2,1,0:T(1,128)S(1)} %bitcast.19), channel_id=1, replica_groups=mesh['slab'=32,'cable'=4] {'slab','cable'}, dimensions={0} | all-to-all | bytes 131072 | tf_op jit(solution)/shard_map/all_to_all | solution.py:511
  88.0 0.0 collective-permute-done.1.below_ref
  88.0 0.0 copy-done.3
  88.0 0.0 copy-done.8
  88.0 0.0 copy-done.10
  88.0 0.0 copy-done.12
  88.1 12.9 %electrics.1 = f32[3,8,128,256]{3,2,1,0:T(8,128)} custom-call(f32[3,8,128,256]{3,2,1,0:T(8,128)S(1)} %copy-done.1, f32[3,8,128,256]{3,2,1,0:T(8,128)S(1)} %copy-done.3, f32[2,128,256]{2,1,0:T(8,128)S(1)} %collective-permute-done.1.below_ref, f32[8,128,256]{2,1,0:T(8,128)S(1)} %copy-done.8, f32[128,128]{1,0:T(8,128)S(1)} %bitcast.14, ...), custom_call_target="tpu_custom_call" | custom-call | tf_op jit(solution)/shard_map/electrics/pallas_call | solution.py:30
  (11 shorter events, 0.0 us)
Async XLA Ops:
  0.6 1.9 %copy-start = (f32[3,8,128,256]{3,2,1,0:T(8,128)S(1)}, f32[3,8,128,256]{3,2,1,0:T(8,128)}, u32[]{:S(2)}) copy-start(f32[3,8,128,256]{3,2,1,0:T(8,128)} %e_ref.5) | copy-start | bytes 9437188
  2.5 0.9 copy-start.9
  3.4 0.8 copy-start.11
  4.3 12.5 %copy-start.1 = (f32[3,8,128,256]{3,2,1,0:T(8,128)S(1)}, f32[3,8,128,256]{3,2,1,0:T(8,128)}, u32[]{:S(2)}) copy-start(f32[3,8,128,256]{3,2,1,0:T(8,128)} %e_ref.5) | copy-start | bytes 9437188
  7.1 40.9 %copy-start.13 = (s32[128]{0:T(128)S(1)}, s32[128]{0:T(128)}, u32[]{:S(2)}) copy-start(s32[128]{0:T(128)} %param.20) | copy-start | bytes 1540
  7.1 9.7 %collective-permute-start = (f32[2,128,256]{2,1,0:T(8,128)S(1)}, f32[2,128,256]{2,1,0:T(8,128)S(1)}, u32[]{:S(2)}, u32[]{:S(2)}) collective-permute-start(f32[2,128,256]{2,1,0:T(8,128)S(1)} %get-tuple-element.15), channel_id=1, source_target_pairs={{1,0},{2,1},{3,2},{4,3},{5,4},{6,5},{7,6},{8,7},{9,8},{10,9},{11,1... | collective-permute-start | bytes 786440 | tf_op jit(solution)/shard_map/ppermute | solution.py:502
  16.8 1.9 %copy-start.2 = (f32[3,8,128,256]{3,2,1,0:T(8,128)S(1)}, f32[3,8,128,256]{3,2,1,0:T(8,128)}, u32[]{:S(2)}) copy-start(f32[3,8,128,256]{3,2,1,0:T(8,128)} %h_ref.1) | copy-start | bytes 9437188
  18.7 29.3 %copy-start.4 = (f32[32,128,128]{2,1,0:T(8,128)S(1)}, f32[32,128,128]{2,1,0:T(8,128)}, u32[]{:S(2)}) copy-start(f32[32,128,128]{2,1,0:T(8,128)} %v_ref.1) | copy-start | bytes 6291460
  18.7 29.3 %copy-start.5 = (f32[32,128,128]{2,1,0:T(8,128)S(1)}, f32[32,128,128]{2,1,0:T(8,128)}, u32[]{:S(2)}) copy-start(f32[32,128,128]{2,1,0:T(8,128)} %i_ref.1) | copy-start | bytes 6291460
  18.7 29.3 %copy-start.6 = (f32[32,32,128]{2,1,0:T(8,128)S(1)}, f32[32,32,128]{2,1,0:T(8,128)}, u32[]{:S(2)}) copy-start(f32[32,32,128]{2,1,0:T(8,128)} %a_ref.3) | copy-start | bytes 1572868
  18.7 29.3 %copy-start.7 = (f32[32,32,128]{2,1,0:T(8,128)S(1)}, f32[32,32,128]{2,1,0:T(8,128)}, u32[]{:S(2)}) copy-start(f32[32,32,128]{2,1,0:T(8,128)} %b_ref.3) | copy-start | bytes 1572868
  21.7 66.3 %collective-permute-start.1 = (f32[2,128,256]{2,1,0:T(8,128)S(1)}, f32[2,128,256]{2,1,0:T(8,128)S(1)}, u32[]{:S(2)}, u32[]{:S(2)}) collective-permute-start(f32[2,128,256]{2,1,0:T(8,128)S(1)} %get-tuple-element.17), channel_id=1, source_target_pairs={{0,1},{1,2},{2,3},{3,4},{4,5},{5,6},{6,7},{7,8},{8,9},{9,10},{10,1... | collective-permute-start | bytes 786440 | tf_op jit(solution)/shard_map/ppermute | solution.py:502
  48.0 23.3 %copy-start.14 = (s32[128]{0:T(128)S(1)}, s32[128]{0:T(128)}, u32[]{:S(2)}) copy-start(s32[128]{0:T(128)} %param.21) | copy-start | bytes 1540
  67.2 4.2 %collective-permute-start.2 = (f32[3,32,128]{2,1,0:T(8,128)S(1)}, f32[3,32,128]{2,1,0:T(8,128)S(1)}, u32[]{:S(2)}, u32[]{:S(2)}) collective-permute-start(f32[3,32,128]{2,1,0:T(8,128)S(1)} %get-tuple-element.19), channel_id=1, source_target_pairs={{0,1},{1,2},{2,3},{3,0},{4,5},{5,6},{6,7},{7,4},{8,9},{9,10},{10,1... | collective-permute-start | bytes 147464 | tf_op jit(solution)/shard_map/ppermute | solution.py:507
  71.3 16.7 %copy-start.3 = (f32[3,8,128,256]{3,2,1,0:T(8,128)S(1)}, f32[3,8,128,256]{3,2,1,0:T(8,128)}, u32[]{:S(2)}) copy-start(f32[3,8,128,256]{3,2,1,0:T(8,128)} %get-tuple-element.12.h_ref) | copy-start | bytes 9437188
  71.3 16.7 %copy-start.8 = (f32[8,128,256]{2,1,0:T(8,128)S(1)}, f32[8,128,256]{2,1,0:T(8,128)}, u32[]{:S(2)}) copy-start(f32[8,128,256]{2,1,0:T(8,128)} %sigma_ref.1) | copy-start | bytes 3145732
  71.3 16.7 %copy-start.10 = (f32[3,1,16384]{2,1,0:T(1,128)S(1)}, f32[3,1,16384]{2,1,0:T(1,128)}, u32[]{:S(2)}) copy-start(f32[3,1,16384]{2,1,0:T(1,128)} %param.18) | copy-start | bytes 589828
  71.3 16.7 %copy-start.12 = (s32[1,16384]{1,0:T(1,128)S(1)}, s32[1,16384]{1,0:T(1,128)}, u32[]{:S(2)}) copy-start(s32[1,16384]{1,0:T(1,128)} %param.19) | copy-start | bytes 196612
where the time goes:
time: 101 us
  Pallas kernels  40.2 us (40%)
  blocking collectives  37.2 us (37%)
  starting transfers between devices  9.82 us (10%)
  waiting for transfers between devices  7.42 us (7%)
  local copies, waits for them, and re-layouts  5.59 us (6%)
    pallas_call x5, Pallas kernels, call(): pl.pallas_call(body, out_shape=out, grid=grid, scratch_shapes=list(scratc...  40.2 us
    all_to_all x2, blocking collectives, exchange(): return lax.all_to_all(x, BOTH, split_axis=0, concat_axis=0, tiled=True)  37.2 us
    ppermute x2, starting transfers between devices, along(): lax.ppermute(x, axis, [(i, i + by) for i in range(peers) if 0 <= i + by <...  9.47 us
    unnamed x30, local copies, waits for them, and re-layouts  5.59 us
    ppermute x1, waiting for transfers between devices, around(): return lax.ppermute(x, axis, [(i, (i + 1) % peers) for i in range(peers)])  3.8 us
    ppermute x2, waiting for transfers between devices, along(): lax.ppermute(x, axis, [(i, i + by) for i in range(peers) if 0 <= i + by <...  3.61 us
  transfers between devices with their start and end apart: 3, of which 2 were waited for; matrix products, arithmetic and copies ran while one was open for 0% of the time, Pallas kernels for 21%

commit v1 on v0

--- a/solution.py
+++ b/solution.py
@@ -21,7 +21,7 @@
     return lax.broadcasted_iota(I32, shape, axis)
 
 
-def call(body, out, *ins, name, scratch=(), limit=40, in_specs=None, aliases=None, out_specs=None, cost=None, grid=()):
+def call(body, out, *ins, name, scratch=(), limit=40, in_specs=None, aliases=None, out_specs=None, micros=None, grid=()):
     kw = {}
     if in_specs is not None:
         kw["in_specs"] = in_specs
@@ -34,7 +34,7 @@
         scratch_shapes=list(scratch),
         input_output_aliases=aliases or {},
         compiler_params=pltpu.CompilerParams(vmem_limit_bytes=limit * MB),
-        cost_estimate=cost,
+        cost_estimate=pl.CostEstimate(flops=0, bytes_accessed=int(micros * 3.69e6), transcendentals=0) if micros else None,
         name=name,
         **kw,
     )(*ins)
@@ -44,8 +44,15 @@
     return jax.ShapeDtypeStruct(dims, dtype)
 
 
-def gather_kernel(e_ref, idx_ref, tan_ref, drive_ref, layer_ref):
-    layer_ref[...] = e_ref[1:3, 0]
+def gather_kernel(e_hbm, idx_hbm, tan_hbm, drive_ref, layer_ref, e_ref, idx_ref, tan_ref, sems):
+    copies = [pltpu.make_async_copy(e_hbm.at[:, x], e_ref.at[:, x], sems.at[x]) for x in range(8)]
+    idx_copy = pltpu.make_async_copy(idx_hbm, idx_ref, sems.at[8])
+    tan_copy = pltpu.make_async_copy(tan_hbm, tan_ref, sems.at[9])
+    idx_copy.start()
+    for copy in copies:
+        copy.start()
+    tan_copy.start()
+    idx_copy.wait()
     for h in range(2):
         lanes = pl.ds(h * 128, 128)
         rows = pl.ds(h, 64, stride=2)
@@ -53,24 +60,48 @@
         idx = [idx[8 * g : 8 * g + 8] for g in range(8)]
         low = [i & 7 for i in idx]
         high = [i >> 3 for i in idx]
-
-        def step(b, acc):
-            acc = list(acc)
-            x = b // 16
-            yrows = pl.ds(pl.multiple_of((b % 16) * 8, 8), 8)
-            src = [e_ref[k, x, yrows, lanes] for k in range(3)]
-            for g in range(8):
-                hit = high[g] == b
-                for k in range(3):
-                    acc[g * 3 + k] = jnp.where(hit, take(src[k], low[g], 0), acc[g * 3 + k])
-            return tuple(acc)
-
-        acc = lax.fori_loop(0, 128, step, (jnp.zeros((8, 128), F),) * 24, unroll=4)
+        acc = (jnp.zeros((8, 128), F),) * 24
+        for x in range(8):
+            if h == 0:
+                copies[x].wait()
+
+            def step(yb, acc):
+                acc = list(acc)
+                yrows = pl.ds(pl.multiple_of(yb * 8, 8), 8)
+                src = [e_ref[k, x, yrows, lanes] for k in range(3)]
+                for g in range(8):
+                    hit = high[g] == yb + 16 * x
+                    for k in range(3):
+                        acc[g * 3 + k] = jnp.where(hit, take(src[k], low[g], 0), acc[g * 3 + k])
+                return tuple(acc)
+
+            acc = lax.fori_loop(0, 16, step, acc, unroll=4)
+        if h == 0:
+            tan_copy.wait()
+            layer_ref[...] = e_ref[1:3, 0]
         picked = [jnp.concatenate([acc[g * 3 + k] for g in range(8)], 0) for k in range(3)]
         steer = [tan_ref[k, rows, :] for k in range(3)]
         drive_ref[rows, :] = steer[0] * picked[0] + steer[1] * picked[1] + steer[2] * picked[2]
 
 
+def samples(electric, cells, steer):
+    return call(
+        gather_kernel,
+        (shape(128, 128), shape(2, 128, 256)),
+        electric, cells, steer,
+        name="samples",
+        in_specs=[pl.BlockSpec(memory_space=pltpu.HBM)] * 3,
+        scratch=[
+            pltpu.VMEM((3, 8, 128, 256), F),
+            pltpu.VMEM((128, 128), I32),
+            pltpu.VMEM((3, 128, 128), F),
+            pltpu.SemaphoreType.DMA((10,)),
+        ],
+        limit=58,
+        micros=4,
+    )
+
+
 def merge_pair(x, y):
     low = iota((8, 128), 0) < 4
     return jnp.where(low, x, pltpu.roll(y, 4, 0)), jnp.where(low, pltpu.roll(x, 4, 0), y)
@@ -82,10 +113,26 @@
 
 
 def line_kernel(
-    v_ref, i_ref, a_ref, b_ref, drive_ref, len_ref,
-    vo_ref, io_ref, ends_ref, ind_ref,
-    vt, it, at, vg, ig, ah, bh, dg, eg, indt,
+    v_hbm, i_hbm, a_hbm, b_hbm, drive_ref, len_ref,
+    vo_hbm, io_hbm, ends_ref, ind_ref,
+    vt, it, at, vg, ig, ah, bh, dg, eg, indt, v_ref, i_ref, a_ref, b_ref, sems, in_sems,
 ):
+    arrivals = []
+    for q in range(4):
+        part = pl.ds(8 * q, 8)
+        pair = [
+            pltpu.make_async_copy(src.at[part], dst.at[part], in_sems.at[2 * q + m])
+            for m, (src, dst) in enumerate(((v_hbm, v_ref), (i_hbm, i_ref)))
+        ]
+        for copy in pair:
+            copy.start()
+        arrivals.append(pair)
+    matrices = [
+        pltpu.make_async_copy(src, dst, in_sems.at[8 + m])
+        for m, (src, dst) in enumerate(((a_hbm, a_ref), (b_hbm, b_ref)))
+    ]
+    for copy in matrices:
+        copy.start()
     sub8 = iota((8, 128), 0)
     lane8 = iota((8, 128), 1)
     lane = iota((128, 128), 1)
@@ -95,7 +142,12 @@
         it[c] = i_ref[c].T
         return carry
 
-    lax.fori_loop(0, 32, turn_in, 0, unroll=4)
+    for q in range(4):
+        for copy in arrivals[q]:
+            copy.wait()
+        lax.fori_loop(8 * q, 8 * q + 8, turn_in, 0, unroll=4)
+    for copy in matrices:
+        copy.wait()
 
     spread = [(sub8 >> 2) + 2 * j for j in range(4)]
     own = (sub8 & 3) == (lane8 & 3)
@@ -128,16 +180,6 @@
 
         lax.fori_loop(0, 16, pack, 0, unroll=2)
 
-    drive_t = drive_ref[...].T
-    at[0] = drive_t
-    at[1] = jnp.broadcast_to(len_ref[...].astype(F), (128, 128)).T
-    for b in range(16):
-        rows = slice(8 * b, 8 * b + 8)
-        for p, value in enumerate(merge_pair(at[0, rows, :], at[0, rows, :])):
-            dg[16 * b + 8 * p : 16 * b + 8 * p + 8, :] = value
-        for p, value in enumerate(merge_pair(at[1, rows, :], at[1, rows, :])):
-            eg[16 * b + 8 * p : 16 * b + 8 * p + 8, :] = value.astype(I32)
-
     def regroup(b, carry):
         rows = pl.ds(pl.multiple_of(b * 8, 8), 8)
         for src, dst in ((vt, vg), (it, ig)):
@@ -148,6 +190,15 @@
         return carry
 
     lax.fori_loop(0, 16, regroup, 0, unroll=2)
+
+    at[0] = drive_ref[...].T
+    at[1] = jnp.broadcast_to(len_ref[...].astype(F), (128, 128)).T
+    for b in range(16):
+        rows = slice(8 * b, 8 * b + 8)
+        for p, value in enumerate(merge_pair(at[0, rows, :], at[0, rows, :])):
+            dg[16 * b + 8 * p : 16 * b + 8 * p + 8, :] = value
+        for p, value in enumerate(merge_pair(at[1, rows, :], at[1, rows, :])):
+            eg[16 * b + 8 * p : 16 * b + 8 * p + 8, :] = value.astype(I32)
 
     def product(m_ref, rows, x):
         high, low = split_parts(x)
@@ -219,31 +270,50 @@
 
     lax.fori_loop(0, 16, ungroup, 0, unroll=2)
 
-    def turn_out(c, carry):
-        vo_ref[c] = vt[c].T
-        io_ref[c] = it[c].T
-        return carry
-
-    lax.fori_loop(0, 32, turn_out, 0, unroll=4)
     ind_ref[...] = indt[...].T
+    copies = []
+    for q in range(4):
+
+        def turn_out(n, carry):
+            c = 8 * q + n
+            vg[pl.ds(pl.multiple_of(c * 128, 128), 128), :] = vt[c].T
+            ig[pl.ds(pl.multiple_of(c * 128, 128), 128), :] = it[c].T
+            return carry
+
+        lax.fori_loop(0, 8, turn_out, 0, unroll=4)
+        part = pl.ds(1024 * q, 1024)
+        for m, (src, dst) in enumerate(((vg, vo_hbm), (ig, io_hbm))):
+            copy = pltpu.make_async_copy(src.at[part], dst.at[part], sems.at[2 * q + m])
+            copy.start()
+            copies.append(copy)
+    for copy in copies:
+        copy.wait()
 
 
 def lines(voltage, current, inductance, capacitance, drive, lengths):
     big = pltpu.VMEM((32, 128, 128), F)
     flat = pltpu.VMEM((4096, 128), F)
     packed = pltpu.VMEM((4096, 256), B16)
-    return call(
+    outside = pl.BlockSpec(memory_space=pltpu.HBM)
+    inside = pl.BlockSpec(memory_space=pltpu.VMEM)
+    volts, amps, ends, induced = call(
         line_kernel,
-        (shape(32, 128, 128), shape(32, 128, 128), shape(3, 32, 128), shape(128, 128)),
+        (shape(4096, 128), shape(4096, 128), shape(3, 32, 128), shape(128, 128)),
         voltage, current, inductance, capacitance, drive, lengths,
         name="lines",
-        scratch=[big, big, big, flat, flat, packed, packed,
-                 pltpu.VMEM((256, 128), F), pltpu.VMEM((256, 128), I32), pltpu.VMEM((128, 128), F)],
-        limit=40,
-    )
-
-
-def junction_kernel(ends_ref, link_ref, a_ref, b_ref, v_ref, i_ref, ind_ref, vo_ref, io_ref, indo_ref, buf):
+        in_specs=[outside] * 4 + [inside] * 2,
+        out_specs=(outside, outside, inside, inside),
+        scratch=[big, big, big, flat, flat, packed, packed, pltpu.VMEM((256, 128), F),
+                 pltpu.VMEM((256, 128), I32), pltpu.VMEM((128, 128), F), big, big,
+                 pltpu.VMEM((32, 32, 128), F), pltpu.VMEM((32, 32, 128), F),
+                 pltpu.SemaphoreType.DMA((8,)), pltpu.SemaphoreType.DMA((10,))],
+        limit=53,
+        micros=18,
+    )
+    return volts.reshape(32, 128, 128), amps.reshape(32, 128, 128), ends, induced
+
+
+def junction_kernel(ends_ref, link_ref, a_ref, b_ref, ind_ref, fix_ref, indo_ref, buf):
     link = jnp.broadcast_to(link_ref[...], (8, 128))
     inflow = [
         jnp.concatenate([take(ends_ref[k, 8 * q : 8 * q + 8, :], link, 1) for q in range(4)], 0)
@@ -269,38 +339,68 @@
     v3a = v2a - apply(b_ref, i3a - f3)
     v3b = v2b - v3c + apply(b_ref, i3a)
     sub8 = iota((8, 128), 0)
-    for c in range(32):
-        row = slice(c, c + 1)
-        add = jnp.where(sub8 == 0, v3a[row], jnp.where(sub8 == 1, v3b[row], jnp.where(sub8 == 2, v3c[row], 0.0)))
-        vo_ref[c] = v_ref[c] + add
-        add = jnp.where(sub8 == 0, i3a[row], jnp.where(sub8 == 1, i3b[row], 0.0))
-        io_ref[c] = i_ref[c] + add
+    for n, value in enumerate((v3a, v3b, v3c, i3a, i3b)):
+        fix_ref[n] = value
     mean_a = jnp.sum(i3a, axis=0, keepdims=True) * (1.0 / 32.0)
     mean_b = jnp.sum(i3b, axis=0, keepdims=True) * (1.0 / 32.0)
     indo_ref[...] = ind_ref[...]
     indo_ref[0:8, :] = ind_ref[0:8, :] + jnp.where(sub8 == 0, mean_a, jnp.where(sub8 == 1, mean_b, 0.0))
 
 
-def junctions(ends, link, inductance, capacitance, volts, amps, induced):
-    head = pl.BlockSpec((32, 8, 128), lambda n: (0, 0, 0))
-    whole = lambda *dims: pl.BlockSpec(dims, lambda n: (0,) * len(dims))
+def junctions(ends, link, inductance, capacitance, induced):
     return call(
         junction_kernel,
-        (shape(32, 128, 128), shape(32, 128, 128), shape(128, 128)),
-        ends, link, inductance, capacitance, volts, amps, induced,
+        (shape(5, 32, 128), shape(128, 128)),
+        ends, link, inductance, capacitance, induced,
         name="junctions",
+        scratch=[pltpu.VMEM((32, 128), F)],
+        limit=3,
+        micros=1,
+    )
+
+
+def finish_kernel(v_ref, i_ref, fix_ref, vo_ref, io_ref):
+    sub8 = iota((8, 128), 0)
+    for c in range(32):
+        fix = [fix_ref[m, c : c + 1, :] for m in range(5)]
+        first, second = sub8 == 0, sub8 == 1
+        vo_ref[c] = v_ref[c] + jnp.where(first, fix[0], jnp.where(second, fix[1], jnp.where(sub8 == 2, fix[2], 0.0)))
+        io_ref[c] = i_ref[c] + jnp.where(first, fix[3], jnp.where(second, fix[4], 0.0))
+
+
+def finish(volts, amps, fix):
+    head = pl.BlockSpec((32, 8, 128), lambda n: (0, 0, 0))
+    return call(
+        finish_kernel,
+        (shape(32, 128, 128), shape(32, 128, 128)),
+        volts, amps, fix,
+        name="finish",
         grid=(1,),
-        in_specs=[whole(3, 32, 128), whole(1, 128), whole(32, 32, 128), whole(32, 32, 128), head, head, whole(128, 128)],
-        out_specs=(head, head, whole(128, 128)),
-        aliases={4: 0, 5: 1},
-        scratch=[pltpu.VMEM((32, 128), F)],
-        limit=16,
-    )
-
-
-def magnetic_kernel(e_ref, h_ref, above_ref, ho_ref, layer_ref):
+        in_specs=[head, head, pl.BlockSpec((5, 32, 128), lambda n: (0, 0, 0))],
+        out_specs=(head, head),
+        aliases={0: 0, 1: 1},
+        limit=8,
+        micros=2,
+    )
+
+
+def magnetic_kernel(e_hbm, h_hbm, above_ref, ho_hbm, layer_ref, e_ref, h_ref, ho_ref, sems):
     sub = iota((8, 256), 0)
     lane = iota((8, 256), 1)
+
+    def fetch(x):
+        return (
+            pltpu.make_async_copy(e_hbm.at[:, x], e_ref.at[:, x], sems.at[0, x]),
+            pltpu.make_async_copy(h_hbm.at[:, x], h_ref.at[:, x], sems.at[1, x]),
+        )
+
+    def store(x):
+        return pltpu.make_async_copy(ho_ref.at[:, x], ho_hbm.at[:, x], sems.at[2, x])
+
+    for x in range(8):
+        for copy in fetch(x):
+            copy.start()
+    fetch(0)[0].wait()
 
     def one_layer(x, carry):
         nx = jnp.minimum(x + 1, 7)
@@ -327,17 +427,36 @@
                 ho_ref[k, x, rows, :] = h_ref[k, x, rows, :] - COURANT * curl[k]
         return carry
 
-    lax.fori_loop(0, 8, one_layer, 0)
+    def layer_step(x, carry):
+        @pl.when(x < 7)
+        def _():
+            fetch(x + 1)[0].wait()
+
+        fetch(x)[1].wait()
+        one_layer(x, carry)
+        store(x).start()
+        return carry
+
+    lax.fori_loop(0, 8, layer_step, 0)
     layer_ref[...] = ho_ref[1:3, 7]
+    for x in range(8):
+        store(x).wait()
 
 
 def magnetics(electric, magnetic, above):
+    whole = pltpu.VMEM((3, 8, 128, 256), F)
+    outside = pl.BlockSpec(memory_space=pltpu.HBM)
+    inside = pl.BlockSpec(memory_space=pltpu.VMEM)
     return call(
         magnetic_kernel,
         (shape(3, 8, 128, 256), shape(2, 128, 256)),
         electric, magnetic, above,
         name="magnetics",
-        limit=24,
+        in_specs=[outside, outside, inside],
+        out_specs=(outside, inside),
+        scratch=[whole, whole, whole, pltpu.SemaphoreType.DMA((3, 8))],
+        limit=53,
+        micros=4,
     )
 
 
@@ -373,10 +492,7 @@
     return keys
 
 
-def electric_kernel(
-    e_ref, h_ref, below_ref, sigma_ref, ind_ref, tan_ref, idx_ref,
-    eo_ref, cell_s, perm_s, val_s, dep_s, plane_s,
-):
+def search_kernel(idx_ref, cell_ref, perm_ref, pos_ref):
     sub8 = iota((8, 128), 0)
     lane8 = iota((8, 128), 1)
     keys = []
@@ -385,31 +501,18 @@
         cell = idx_ref[8 * n : 8 * n + 8, :]
         keys.append(((owner & 1) * 1024 + cell) * 128 + owner)
     keys = jnp.concatenate(sort_columns(keys), 0).T
-    cell_s[...] = keys >> 7
-    perm_s[...] = keys & 127
-
-    for k in range(3):
-        val_s[k] = (tan_ref[k] * ind_ref[...]).T
-    for n in range(16):
-        rows = slice(8 * n, 8 * n + 8)
-        perm = perm_s[rows, :]
-        cell = cell_s[rows, :]
-        val = [take(val_s[k, rows, :], perm, 1) for k in range(3)]
-        for gap in (1, 2, 4, 8, 16, 32):
-            same = pltpu.roll(cell, gap, 1) == cell
-            val = [v + jnp.where(same, pltpu.roll(v, gap, 1), 0.0) for v in val]
-        for k in range(3):
-            val_s[k, rows, :] = val[k]
+    cell_ref[...] = keys >> 7
+    perm_ref[...] = keys & 127
 
     def spread(n, carry):
         rows = pl.ds(pl.multiple_of(n * 8, 8), 8)
-        cell = cell_s[rows, :]
-        val = [val_s[k, rows, :] for k in range(3)]
+        cell = cell_ref[rows, :]
         for h in range(2):
             fence = {
                 p: take(cell, jnp.full((8, 128), 64 * h + p, I32), 1)
                 for p in (0, 8, 16, 24, 32, 40, 48, 56)
             }
+            chains = []
             for x in range(8):
                 target = lane8 + (h * 1024 + x * 128)
                 up = fence[32] <= target
@@ -425,19 +528,59 @@
                     jnp.where(up2, fence[24], fence[8]),
                 )
                 hit = probe <= target
-                pos = jnp.where(hit, pos + 8, pos)
-                cur = jnp.where(hit, probe, cur)
-                for step in (4, 2, 1):
-                    probe = take(cell, pos + step, 1)
-                    hit = probe <= target
-                    pos = jnp.where(hit, pos + step, pos)
-                    cur = jnp.where(hit, probe, cur)
-                found = cur == target
-                for k in range(3):
-                    dep_s[h, k, x, rows, :] = jnp.where(found, take(val[k], pos, 1), 0.0)
+                chains.append((target, jnp.where(hit, pos + 8, pos), jnp.where(hit, probe, cur)))
+            for step in (4, 2, 1):
+                probes = [take(cell, pos + step, 1) for _, pos, _ in chains]
+                hits = [probe <= chain[0] for probe, chain in zip(probes, chains)]
+                chains = [
+                    (target, jnp.where(hit, pos + step, pos), jnp.where(hit, probe, cur))
+                    for (target, pos, cur), probe, hit in zip(chains, probes, hits)
+                ]
+            for x, (target, pos, cur) in enumerate(chains):
+                pos_ref[h, x, rows, :] = jnp.where(cur == target, pos, -1)
         return carry
 
     lax.fori_loop(0, 16, spread, 0)
+
+
+def search(cells):
+    return call(
+        search_kernel,
+        (shape(128, 128, dtype=I32), shape(128, 128, dtype=I32), shape(2, 8, 128, 128, dtype=I32)),
+        cells,
+        name="search",
+        limit=4,
+        micros=4,
+    )
+
+
+def electric_kernel(
+    e_hbm, h_hbm, below_ref, sigma_hbm, ind_ref, tan_ref, cell_s, perm_s, pos_hbm,
+    eo_hbm, val_s, plane_s, eo_ref, e_ref, h_ref, sigma_ref, pos_ref, sems, in_sems,
+):
+    def fetch(x):
+        return (
+            pltpu.make_async_copy(pos_hbm.at[:, x], pos_ref.at[:, x], in_sems.at[0, x]),
+            pltpu.make_async_copy(h_hbm.at[:, x], h_ref.at[:, x], in_sems.at[1, x]),
+            pltpu.make_async_copy(e_hbm.at[:, x], e_ref.at[:, x], in_sems.at[2, x]),
+            pltpu.make_async_copy(sigma_hbm.at[x], sigma_ref.at[x], in_sems.at[3, x]),
+        )
+
+    for x in range(8):
+        for copy in fetch(x):
+            copy.start()
+    for k in range(3):
+        val_s[k] = (tan_ref[k] * ind_ref[...]).T
+    for n in range(16):
+        rows = slice(8 * n, 8 * n + 8)
+        perm = perm_s[rows, :]
+        cell = cell_s[rows, :]
+        val = [take(val_s[k, rows, :], perm, 1) for k in range(3)]
+        for gap in (1, 2, 4, 8, 16, 32):
+            same = pltpu.roll(cell, gap, 1) == cell
+            val = [v + jnp.where(same, pltpu.roll(v, gap, 1), 0.0) for v in val]
+        for k in range(3):
+            val_s[k, rows, :] = val[k]
 
     sub = iota((8, 256), 0)
     lane = iota((8, 256), 1)
@@ -445,9 +588,16 @@
     def one_layer(x, carry):
         px = jnp.maximum(x - 1, 0)
         first = x == 0
-        for k in range(3):
-            for h in range(2):
-                plane_s[k, :, 128 * h : 128 * h + 128] = dep_s[h, k, x].T
+        for h in range(2):
+            tiles = [[], [], []]
+            for n in range(16):
+                pos = pos_ref[h, x, 8 * n : 8 * n + 8, :]
+                spot = pos & 127
+                for k in range(3):
+                    picked = take(val_s[k, 8 * n : 8 * n + 8, :], spot, 1)
+                    tiles[k].append(jnp.where(pos >= 0, picked, 0.0))
+            for k in range(3):
+                plane_s[k, :, 128 * h : 128 * h + 128] = jnp.concatenate(tiles[k], 0).T
         for yb in range(16):
             rows = slice(8 * yb, 8 * yb + 8)
             m = [h_ref[k, x, rows, :] for k in range(3)]
@@ -474,23 +624,40 @@
                 eo_ref[k, x, rows, :] = keep * e_ref[k, x, rows, :] + push * (curl[k] - plane_s[k, rows, :])
         return carry
 
-    lax.fori_loop(0, 8, one_layer, 0)
-
-
-def electrics(electric, magnetic_new, below, conductivity, induced, tangent, cells):
+    def send_layer(x, carry):
+        for copy in fetch(x):
+            copy.wait()
+        one_layer(x, carry)
+        pltpu.make_async_copy(eo_ref.at[:, x], eo_hbm.at[:, x], sems.at[x]).start()
+        return carry
+
+    lax.fori_loop(0, 8, send_layer, 0)
+    for x in range(8):
+        pltpu.make_async_copy(eo_ref.at[:, x], eo_hbm.at[:, x], sems.at[x]).wait()
+
+
+def electrics(electric, magnetic_new, below, conductivity, induced, tangent, found):
+    whole = pltpu.VMEM((3, 8, 128, 256), F)
+    outside = pl.BlockSpec(memory_space=pltpu.HBM)
+    inside = pl.BlockSpec(memory_space=pltpu.VMEM)
     return call(
         electric_kernel,
         shape(3, 8, 128, 256),
-        electric, magnetic_new, below, conductivity, induced, tangent, cells,
+        electric, magnetic_new, below, conductivity, induced, tangent, *found,
         name="electrics",
+        in_specs=[outside, outside, inside, outside, inside, inside, inside, inside, outside],
+        out_specs=outside,
         scratch=[
-            pltpu.VMEM((128, 128), I32),
-            pltpu.VMEM((128, 128), I32),
             pltpu.VMEM((3, 128, 128), F),
-            pltpu.VMEM((2, 3, 8, 128, 128), F),
             pltpu.VMEM((3, 128, 256), F),
+            whole, whole, whole,
+            pltpu.VMEM((8, 128, 256), F),
+            pltpu.VMEM((2, 8, 128, 128), I32),
+            pltpu.SemaphoreType.DMA((8,)),
+            pltpu.SemaphoreType.DMA((4, 8)),
         ],
-        limit=30,
+        limit=53,
+        micros=6,
     )
 
 
@@ -517,22 +684,25 @@
 ):
     cells = sample_cell.reshape(128, 128)
     steer = tangent.reshape(3, 128, 128)
-    drive_local, layer = call(
-        gather_kernel, (shape(128, 128), shape(2, 128, 256)), electric, cells, steer, name="gather", limit=20
-    )
+    drive_local, layer = samples(electric, cells, steer)
     above = along(layer, BOTH, -1)
     drive = exchange(drive_local)
+    magnetic_new, layer = magnetics(electric, magnetic, above)
+    drive, layer = lax.optimization_barrier((drive, layer))
+    below = along(layer, BOTH, 1)
     volts, amps, ends, induced = lines(
         voltage, current, inverse_inductance, inverse_capacitance, drive, tube_length.reshape(1, 128)
     )
+    ends, cells = lax.optimization_barrier((ends, cells))
     ends = around(ends, "cable")
-    magnetic_new, layer = magnetics(electric, magnetic, above)
-    below = along(layer, BOTH, 1)
-    volts, amps, induced = junctions(
-        ends, junction_link.reshape(1, 128), inverse_inductance, inverse_capacitance, volts, amps, induced
-    )
+    found = search(cells)
+    fix, induced = junctions(
+        ends, junction_link.reshape(1, 128), inverse_inductance, inverse_capacitance, induced
+    )
+    induced, found = lax.optimization_barrier((induced, found))
     induced_local = exchange(induced)
-    electric_new = electrics(electric, magnetic_new, below, conductivity, induced_local, steer, cells)
+    volts, amps = finish(volts, amps, fix)
+    electric_new = electrics(electric, magnetic_new, below, conductivity, induced_local, steer, found)
     return electric_new, magnetic_new, volts, amps
 
 

time: 101 us -> 84 us (0.83)
  blocking collectives: 37.2 us -> 0 us
  starting transfers between devices: 9.82 us -> 24.9 us
  waiting for transfers between devices: 7.42 us -> 13.2 us
  local copies, waits for them, and re-layouts: 5.59 us -> 0.04 us
  Pallas kernels: 40.2 us -> 44.8 us
    all_to_all x2 -> x0, blocking collectives: 37.2 us -> none  [exchange(): return lax.all_to_all(x, BOTH, split_axis=0, concat_axis=0, tiled=True)]
    all_to_all x0 -> x2, starting transfers between devices: none -> 16.5 us  [exchange(): return lax.all_to_all(x, BOTH, split_axis=0, concat_axis=0, tiled=True)]
    all_to_all x0 -> x2, waiting for transfers between devices: none -> 13.2 us  [exchange(): return lax.all_to_all(x, BOTH, split_axis=0, concat_axis=0, tiled=True)]
    unnamed x30 -> x14, local copies, waits for them, and re-layouts: 5.59 us -> 0.04 us
    pallas_call x5 -> x7, Pallas kernels: 40.2 us -> 44.8 us  [call(): pl.pallas_call(body, out_shape=out, grid=grid, scratch_shapes=list(scratc...]
    ppermute x1, waiting for transfers between devices: 3.8 us -> 0.01 us  [around(): return lax.ppermute(x, axis, [(i, (i + 1) % peers) for i in range(peers)])]
    ppermute x2, waiting for transfers between devices: 3.61 us -> 0.01 us  [along(): lax.ppermute(x, axis, [(i, i + by) for i in range(peers) if 0 <= i + by <...]
    ppermute x2, starting transfers between devices: 9.47 us -> 8.28 us  [along(): lax.ppermute(x, axis, [(i, i + by) for i in range(peers) if 0 <= i + by <...]
  transfers between devices with their start and end apart: 3 -> 5, of which waited for: 2 -> 2; matrix products, arithmetic and copies ran while one was open for 0% -> 0% of each run, Pallas kernels for 21% -> 40%
where the time goes in v1:
time: 84 us; the launch traced here: 83.8 us
  Pallas kernels  44.8 us (53%)
  starting transfers between devices  24.9 us (30%)
  waiting for transfers between devices  13.2 us (16%)
    pallas_call x7, Pallas kernels, call(): pl.pallas_call(body, out_shape=out, grid=grid, scratch_shapes=list(scratc...  44.8 us
    all_to_all x2, starting transfers between devices, exchange(): return lax.all_to_all(x, BOTH, split_axis=0, concat_axis=0, tiled=True)  16.5 us
    all_to_all x2, waiting for transfers between devices, exchange(): return lax.all_to_all(x, BOTH, split_axis=0, concat_axis=0, tiled=True)  13.2 us
    ppermute x2, starting transfers between devices, along(): lax.ppermute(x, axis, [(i, i + by) for i in range(peers) if 0 <= i + by <...  8.28 us
  transfers between devices with their start and end apart: 5, of which 2 were waited for; matrix products, arithmetic and copies ran while one was open for 0% of the time, Pallas kernels for 40%

profile of v1, /device:TPU:1, one launch (start us, length us, event | category | flops | bytes accessed | tf_op | source)
XLA Modules:
  0.0 83.8 jit_solution(4186486362567265443)
XLA Ops:
  0.6 4.3 %samples.1 = (f32[128,128]{1,0:T(8,128)}, f32[2,128,256]{2,1,0:T(8,128)}) custom-call(f32[3,8,128,256]{3,2,1,0:T(8,128)} %e_hbm.5, s32[128,128]{1,0:T(8,128)} %bitcast.18, f32[3,128,128]{2,1,0:T(8,128)} %bitcast.14), custom_call_target="tpu_custom_call" | custom-call | bytes 14760000 | tf_op jit(solution)/shard_map/samples/pallas_call | solution.py:30
  4.9 6.0 %collective-permute-start = (f32[2,128,256]{2,1,0:T(8,128)}, f32[2,128,256]{2,1,0:T(8,128)S(1)}, u32[]{:S(2)}, u32[]{:S(2)}) collective-permute-start(f32[2,128,256]{2,1,0:T(8,128)} %get-tuple-element.27), channel_id=1, source_target_pairs={{1,0},{2,1},{3,2},{4,3},{5,4},{6,5},{7,6},{8,7},{9,8},{10,9},{11,1... | collective-permute-start | bytes 786440 | tf_op jit(solution)/shard_map/ppermute | solution.py:669
  10.9 7.9 %all-to-all-start = ((f32[128,1,128]{2,1,0:T(1,128)}), f32[128,1,128]{2,1,0:T(1,128)S(1)}, u32[]{:S(2)}, u32[]{:S(2)}) async-start(f32[128,1,128]{2,1,0:T(1,128)} %bitcast.24), calls=%async_computation | async-start | bytes 131072 | tf_op jit(solution)/shard_map/all_to_all | solution.py:678
  18.9 0.0 copy-start
  18.9 0.0 copy-start.5
  18.9 0.0 collective-permute-done.above_ref
  18.9 4.6 %magnetics.1 = (f32[3,8,128,256]{3,2,1,0:T(8,128)}, f32[2,128,256]{2,1,0:T(8,128)S(1)}) custom-call(f32[3,8,128,256]{3,2,1,0:T(8,128)} %e_hbm.5, f32[3,8,128,256]{3,2,1,0:T(8,128)} %h_hbm.1, f32[2,128,256]{2,1,0:T(8,128)S(1)} %collective-permute-done.above_ref), custom_call_target="tpu_custom_call" | custom-call | bytes 14760000 | tf_op jit(solution)/shard_map/magnetics/pallas_call | solution.py:30
  23.6 5.2 %all-to-all-done = f32[128,1,128]{2,1,0:T(1,128)S(1)} async-done(((f32[128,1,128]{2,1,0:T(1,128)}), f32[128,1,128]{2,1,0:T(1,128)S(1)}, u32[]{:S(2)}, u32[]{:S(2)}) %all-to-all-start) | async-done | bytes 65568 | tf_op jit(solution)/shard_map/all_to_all | solution.py:678
  28.7 2.2 %collective-permute-start.1 = (f32[2,128,256]{2,1,0:T(8,128)S(1)}, f32[2,128,256]{2,1,0:T(8,128)S(1)}, u32[]{:S(2)}, u32[]{:S(2)}) collective-permute-start(f32[2,128,256]{2,1,0:T(8,128)S(1)} %get-tuple-element.31), channel_id=1, source_target_pairs={{0,1},{1,2},{2,3},{3,4},{4,5},{5,6},{6,7},{7,8},{8,9},{9,10},{10,1... | collective-permute-start | bytes 786440 | tf_op jit(solution)/shard_map/ppermute | solution.py:669
  31.0 0.0 copy-done
  31.0 0.0 copy-done.5
  31.0 0.0 copy-start.4
  31.0 0.0 copy-start.1
  31.0 0.0 copy-start.6
  31.0 19.6 %lines.1 = (f32[4096,128]{1,0:T(8,128)}, f32[4096,128]{1,0:T(8,128)}, f32[3,32,128]{2,1,0:T(8,128)S(1)}, f32[128,128]{1,0:T(8,128)S(1)}) custom-call(f32[32,128,128]{2,1,0:T(8,128)} %v_hbm.1, f32[32,128,128]{2,1,0:T(8,128)} %i_hbm.1, f32[32,32,128]{2,1,0:T(8,128)S(1)} %copy-done, f32[32,32,128]{2,1,0:T(8,128)} %b_ref.1, f32[128,128]{1,0:T(8,128)S(1)} %bitcast.17, ...), custom_call_target="tpu_custom_call" | custom-call | bytes 66420000 | tf_op jit(solution)/shard_map/lines/pallas_call | solution.py:30
  50.6 0.1 collective-permute-start.2
  50.7 0.0 copy-done.4
  50.7 6.1 %search.1 = (s32[128,128]{1,0:T(8,128)S(1)}, s32[128,128]{1,0:T(8,128)S(1)}, s32[2,8,128,128]{3,2,1,0:T(8,128)S(1)}) custom-call(s32[128,128]{1,0:T(8,128)S(1)} %bitcast.19), custom_call_target="tpu_custom_call" | custom-call | bytes 14760000 | tf_op jit(solution)/shard_map/search/pallas_call | solution.py:30
  56.8 0.0 copy-start.2
  56.8 0.0 collective-permute-done.2.ends_ref
  56.8 0.0 copy-done.1
  56.8 0.0 copy-done.6
  56.9 1.1 %junctions.1 = (f32[5,32,128]{2,1,0:T(8,128)S(1)}, f32[128,128]{1,0:T(8,128)}) custom-call(f32[3,32,128]{2,1,0:T(8,128)S(1)} %collective-permute-done.2.ends_ref, s32[1,128]{1,0:T(1,128)S(1)} %bitcast.21, f32[32,32,128]{2,1,0:T(8,128)S(1)} %copy-done, f32[32,32,128]{2,1,0:T(8,128)S(1)} %copy-done.1, f32[128,128]{1,0:T(8,128)S(1)} %get-tuple-element.35.ind_ref), custom_call_target="tpu_custom_call" | custom-call | bytes 3690000 | tf_op jit(solution)/shard_map/junctions/pallas_call | solution.py:30
  57.9 0.0 copy-done.2
  57.9 8.6 %all-to-all-start.1 = ((f32[128,1,128]{2,1,0:T(1,128)}), f32[128,1,128]{2,1,0:T(1,128)S(1)}, u32[]{:S(2)}, u32[]{:S(2)}) async-start(f32[128,1,128]{2,1,0:T(1,128)} %bitcast.8), calls=%async_computation.1 | async-start | bytes 131072 | tf_op jit(solution)/shard_map/all_to_all | solution.py:678
  66.5 0.0 copy-start.3
  66.6 1.8 %finish.1 = (f32[32,128,128]{2,1,0:T(8,128)}, f32[32,128,128]{2,1,0:T(8,128)}) custom-call(f32[32,128,128]{2,1,0:T(8,128)} %bitcast.22, f32[32,128,128]{2,1,0:T(8,128)} %bitcast.23, f32[5,32,128]{2,1,0:T(8,128)S(1)} %get-tuple-element.47.fix_ref), custom_call_target="tpu_custom_call", output_to_operand_aliasing={{0}: (0, {}), {1}: (1, {})} | custom-call | bytes 7380000 | tf_op jit(solution)/shard_map/finish/pallas_call | solution.py:30
  68.3 8.0 %all-to-all-done.1 = f32[128,1,128]{2,1,0:T(1,128)S(1)} async-done(((f32[128,1,128]{2,1,0:T(1,128)}), f32[128,1,128]{2,1,0:T(1,128)S(1)}, u32[]{:S(2)}, u32[]{:S(2)}) %all-to-all-start.1) | async-done | bytes 65568 | tf_op jit(solution)/shard_map/all_to_all | solution.py:678
  76.4 0.0 collective-permute-done.1.below_ref
  76.4 0.0 copy-done.3
  76.4 7.4 %electrics.1 = f32[3,8,128,256]{3,2,1,0:T(8,128)} custom-call(f32[3,8,128,256]{3,2,1,0:T(8,128)} %e_hbm.5, f32[3,8,128,256]{3,2,1,0:T(8,128)} %get-tuple-element.24.h_hbm, f32[2,128,256]{2,1,0:T(8,128)S(1)} %collective-permute-done.1.below_ref, f32[8,128,256]{2,1,0:T(8,128)} %sigma_hbm.1, f32[128,128]{1,0:T(8,128)S(1)} %bitcast.16, ...), custom_call_target="tpu_custom_call" | custom-call | bytes 22140000 | tf_op jit(solution)/shard_map/electrics/pallas_call | solution.py:30
Async XLA Ops:
  4.9 14.0 %collective-permute-start = (f32[2,128,256]{2,1,0:T(8,128)}, f32[2,128,256]{2,1,0:T(8,128)S(1)}, u32[]{:S(2)}, u32[]{:S(2)}) collective-permute-start(f32[2,128,256]{2,1,0:T(8,128)} %get-tuple-element.27), channel_id=1, source_target_pairs={{1,0},{2,1},{3,2},{4,3},{5,4},{6,5},{7,6},{8,7},{9,8},{10,9},{11,1... | collective-permute-start | bytes 786440 | tf_op jit(solution)/shard_map/ppermute | solution.py:669
  10.9 17.8 %all-to-all-start = ((f32[128,1,128]{2,1,0:T(1,128)}), f32[128,1,128]{2,1,0:T(1,128)S(1)}, u32[]{:S(2)}, u32[]{:S(2)}) async-start(f32[128,1,128]{2,1,0:T(1,128)} %bitcast.24), calls=%async_computation | async-start | bytes 131072 | tf_op jit(solution)/shard_map/all_to_all | solution.py:678
  18.9 12.1 %copy-start = (f32[32,32,128]{2,1,0:T(8,128)S(1)}, f32[32,32,128]{2,1,0:T(8,128)}, u32[]{:S(2)}) copy-start(f32[32,32,128]{2,1,0:T(8,128)} %a_ref.1) | copy-start | bytes 1572868
  18.9 12.1 %copy-start.5 = (s32[128]{0:T(128)S(1)}, s32[128]{0:T(128)}, u32[]{:S(2)}) copy-start(s32[128]{0:T(128)} %param.20) | copy-start | bytes 1540
  28.7 47.7 %collective-permute-start.1 = (f32[2,128,256]{2,1,0:T(8,128)S(1)}, f32[2,128,256]{2,1,0:T(8,128)S(1)}, u32[]{:S(2)}, u32[]{:S(2)}) collective-permute-start(f32[2,128,256]{2,1,0:T(8,128)S(1)} %get-tuple-element.31), channel_id=1, source_target_pairs={{0,1},{1,2},{2,3},{3,4},{4,5},{5,6},{6,7},{7,8},{8,9},{9,10},{10,1... | collective-permute-start | bytes 786440 | tf_op jit(solution)/shard_map/ppermute | solution.py:669
  31.0 19.7 %copy-start.4 = (s32[1,16384]{1,0:T(1,128)S(1)}, s32[1,16384]{1,0:T(1,128)}, u32[]{:S(2)}) copy-start(s32[1,16384]{1,0:T(1,128)} %param.19) | copy-start | bytes 196612
  31.0 25.8 %copy-start.1 = (f32[32,32,128]{2,1,0:T(8,128)S(1)}, f32[32,32,128]{2,1,0:T(8,128)}, u32[]{:S(2)}) copy-start(f32[32,32,128]{2,1,0:T(8,128)} %b_ref.1) | copy-start | bytes 1572868
  31.0 25.8 %copy-start.6 = (s32[128]{0:T(128)S(1)}, s32[128]{0:T(128)}, u32[]{:S(2)}) copy-start(s32[128]{0:T(128)} %param.21) | copy-start | bytes 1540
  50.6 6.2 %collective-permute-start.2 = (f32[3,32,128]{2,1,0:T(8,128)S(1)}, f32[3,32,128]{2,1,0:T(8,128)S(1)}, u32[]{:S(2)}, u32[]{:S(2)}) collective-permute-start(f32[3,32,128]{2,1,0:T(8,128)S(1)} %get-tuple-element.34), channel_id=1, source_target_pairs={{0,1},{1,2},{2,3},{3,0},{4,5},{5,6},{6,7},{7,4},{8,9},{9,10},{10,1... | collective-permute-start | bytes 147464 | tf_op jit(solution)/shard_map/ppermute | solution.py:674
  56.8 1.1 %copy-start.2 = (s32[2,8,128,128]{3,2,1,0:T(8,128)}, s32[2,8,128,128]{3,2,1,0:T(8,128)S(1)}, u32[]{:S(2)}) copy-start(s32[2,8,128,128]{3,2,1,0:T(8,128)S(1)} %get-tuple-element.44.pos_hbm) | copy-start | bytes 3145732
  57.9 18.4 %all-to-all-start.1 = ((f32[128,1,128]{2,1,0:T(1,128)}), f32[128,1,128]{2,1,0:T(1,128)S(1)}, u32[]{:S(2)}, u32[]{:S(2)}) async-start(f32[128,1,128]{2,1,0:T(1,128)} %bitcast.8), calls=%async_computation.1 | async-start | bytes 131072 | tf_op jit(solution)/shard_map/all_to_all | solution.py:678
  66.5 9.8 %copy-start.3 = (f32[3,1,16384]{2,1,0:T(1,128)S(1)}, f32[3,1,16384]{2,1,0:T(1,128)}, u32[]{:S(2)}) copy-start(f32[3,1,16384]{2,1,0:T(1,128)} %param.18) | copy-start | bytes 589828

commit v2 on v1

--- a/solution.py
+++ b/solution.py
@@ -112,11 +112,25 @@
     return high, (x - high.astype(F)).astype(B16)
 
 
+def product(m_ref, rows, x):
+    high, low = split_parts(x)
+    rhs = jnp.concatenate([high, low], 1)
+    rhs = jnp.concatenate([rhs, rhs], 0)
+    y = jnp.dot(m_ref[rows, :], rhs, preferred_element_type=F)
+    return y[:, :128] + y[:, 128:]
+
+
 def line_kernel(
     v_hbm, i_hbm, a_hbm, b_hbm, drive_ref, len_ref,
-    vo_hbm, io_hbm, ends_ref, ind_ref,
-    vt, it, at, vg, ig, ah, bh, dg, eg, indt, v_ref, i_ref, a_ref, b_ref, sems, in_sems,
+    vo_hbm, io_hbm, bo_hbm, eg, ends_ref, ind_ref,
+    vt, it, at, vg, ig, ah, bh, dg, indt, v_ref, i_ref, a_ref, b_ref, sems, in_sems,
 ):
+    matrices = [
+        pltpu.make_async_copy(src, dst, in_sems.at[8 + m])
+        for m, (src, dst) in enumerate(((a_hbm, a_ref), (b_hbm, b_ref)))
+    ]
+    for copy in matrices:
+        copy.start()
     arrivals = []
     for q in range(4):
         part = pl.ds(8 * q, 8)
@@ -127,31 +141,15 @@
         for copy in pair:
             copy.start()
         arrivals.append(pair)
-    matrices = [
-        pltpu.make_async_copy(src, dst, in_sems.at[8 + m])
-        for m, (src, dst) in enumerate(((a_hbm, a_ref), (b_hbm, b_ref)))
-    ]
-    for copy in matrices:
-        copy.start()
     sub8 = iota((8, 128), 0)
     lane8 = iota((8, 128), 1)
     lane = iota((128, 128), 1)
 
-    def turn_in(c, carry):
-        vt[c] = v_ref[c].T
-        it[c] = i_ref[c].T
-        return carry
-
-    for q in range(4):
-        for copy in arrivals[q]:
-            copy.wait()
-        lax.fori_loop(8 * q, 8 * q + 8, turn_in, 0, unroll=4)
-    for copy in matrices:
-        copy.wait()
 
     spread = [(sub8 >> 2) + 2 * j for j in range(4)]
     own = (sub8 & 3) == (lane8 & 3)
-    for m_ref, dst in ((a_ref, ah), (b_ref, bh)):
+    for m_ref, dst, arrival in ((a_ref, ah, matrices[0]), (b_ref, bh, matrices[1])):
+        arrival.wait()
 
         def expand(c, carry):
             tiles = []
@@ -180,6 +178,18 @@
 
         lax.fori_loop(0, 16, pack, 0, unroll=2)
 
+    results = [pltpu.make_async_copy(bh, bo_hbm, sems.at[0])]
+    results[0].start()
+
+    def turn_in(c, carry):
+        vt[c] = v_ref[c].T
+        it[c] = i_ref[c].T
+        return carry
+
+    for q in range(4):
+        for copy in arrivals[q]:
+            copy.wait()
+        lax.fori_loop(8 * q, 8 * q + 8, turn_in, 0, unroll=4)
     def regroup(b, carry):
         rows = pl.ds(pl.multiple_of(b * 8, 8), 8)
         for src, dst in ((vt, vg), (it, ig)):
@@ -199,13 +209,6 @@
             dg[16 * b + 8 * p : 16 * b + 8 * p + 8, :] = value
         for p, value in enumerate(merge_pair(at[1, rows, :], at[1, rows, :])):
             eg[16 * b + 8 * p : 16 * b + 8 * p + 8, :] = value.astype(I32)
-
-    def product(m_ref, rows, x):
-        high, low = split_parts(x)
-        rhs = jnp.concatenate([high, low], 1)
-        rhs = jnp.concatenate([rhs, rhs], 0)
-        y = jnp.dot(m_ref[rows, :], rhs, preferred_element_type=F)
-        return y[:, :128] + y[:, 128:]
 
     unroll = 16
     for substep in range(SUB):
@@ -238,6 +241,9 @@
                 out = jnp.where((sub8 >> 1) == i, take(acc[4 * q + i], pick, 0), out)
             ends_ref[substep, 8 * q : 8 * q + 8, :] = out
 
+        if substep == SUB - 1:
+            break
+
         def voltage_step(n, carry):
             for u in range(unroll):
                 g = n * unroll + u
@@ -251,39 +257,93 @@
             return carry
 
         lax.fori_loop(0, 32 // unroll, voltage_step, 0)
+        if substep == SUB - 2:
+            results.append(pltpu.make_async_copy(vg, vo_hbm, sems.at[1]))
+            results[1].start()
+
+    results.append(pltpu.make_async_copy(ig, io_hbm, sems.at[2]))
+    results[2].start()
+
+    def average(b, carry):
+        totals = []
+        for p in range(2):
+            tiles = [ig[pl.ds(pl.multiple_of(b * 256 + 128 * p + 8 * i, 8), 8), :] for i in range(16)]
+            while len(tiles) > 1:
+                tiles = [x + y for x, y in zip(tiles[::2], tiles[1::2])]
+            totals.append(tiles[0] + pltpu.roll(tiles[0], 4, 0))
+        indt[pl.ds(pl.multiple_of(b * 8, 8), 8), :] = jnp.where(sub8 < 4, totals[0], totals[1]) * (1.0 / 32.0)
+        return carry
+
+    lax.fori_loop(0, 16, average, 0, unroll=4)
+    ind_ref[...] = indt[...].T
+    for copy in results:
+        copy.wait()
+
+
+def last_kernel(
+    v_hbm, i_hbm, b_hbm, eg, fix_ref,
+    vo_hbm, io_hbm,
+    vt, it, vg, ig, bh, vo_ref, io_ref, sems, in_sems,
+):
+    sub8 = iota((8, 128), 0)
+    lane8 = iota((8, 128), 1)
+    lane = iota((128, 128), 1)
+    arrivals = []
+    for q in range(4):
+        part = pl.ds(1024 * q, 1024)
+        group = [
+            pltpu.make_async_copy(src.at[part], dst.at[part], in_sems.at[m, q])
+            for m, (src, dst) in enumerate(((i_hbm, ig), (b_hbm, bh), (v_hbm, vg)))
+        ]
+        for copy in group:
+            copy.start()
+        arrivals.append(group)
+
+    for q in range(4):
+        for copy in arrivals[q]:
+            copy.wait()
+        for u in range(8):
+            g = q * 8 + u
+            rows = slice(g * 128, g * 128 + 128)
+            live = jnp.concatenate([lane8 < eg[8 * g : 8 * g + 8, :]] * 16, 0)
+            amps = ig[rows, :]
+            behind = jnp.where(lane == 0, 0.0, pltpu.roll(amps, 1, 1))
+            y = product(bh, rows, amps - behind)
+            vg[rows, :] = jnp.where(live, vg[rows, :] - y, 0.0)
 
     def ungroup(b, carry):
         rows = pl.ds(pl.multiple_of(b * 8, 8), 8)
         for src, dst in ((vg, vt), (ig, it)):
-            sums = [None, None]
             for i in range(16):
                 g0 = src[pl.ds(pl.multiple_of(b * 256 + 8 * i, 8), 8), :]
                 g1 = src[pl.ds(pl.multiple_of(b * 256 + 128 + 8 * i, 8), 8), :]
-                c0, c1 = merge_pair(g0, g1)
-                dst[2 * i, rows, :] = c0
-                dst[2 * i + 1, rows, :] = c1
-                if src is ig:
-                    sums = [c0 + c1 if s is None else s + c0 + c1 for s in sums[:1]] + [None]
-            if src is ig:
-                indt[rows, :] = sums[0] * (1.0 / 32.0)
+                dst[2 * i, rows, :], dst[2 * i + 1, rows, :] = merge_pair(g0, g1)
         return carry
 
     lax.fori_loop(0, 16, ungroup, 0, unroll=2)
-
-    ind_ref[...] = indt[...].T
     copies = []
     for q in range(4):
 
         def turn_out(n, carry):
             c = 8 * q + n
-            vg[pl.ds(pl.multiple_of(c * 128, 128), 128), :] = vt[c].T
-            ig[pl.ds(pl.multiple_of(c * 128, 128), 128), :] = it[c].T
+            row = pl.ds(c, 1)
+            v = vt[c].T
+            i = it[c].T
+            first = sub8 == 0
+            second = sub8 == 1
+            fix = [fix_ref[m, row, :] for m in range(5)]
+            vo_ref[c] = v
+            io_ref[c] = i
+            vo_ref[c, 0:8, :] = v[0:8] + jnp.where(
+                first, fix[0], jnp.where(second, fix[1], jnp.where(sub8 == 2, fix[2], 0.0))
+            )
+            io_ref[c, 0:8, :] = i[0:8] + jnp.where(first, fix[3], jnp.where(second, fix[4], 0.0))
             return carry
 
         lax.fori_loop(0, 8, turn_out, 0, unroll=4)
-        part = pl.ds(1024 * q, 1024)
-        for m, (src, dst) in enumerate(((vg, vo_hbm), (ig, io_hbm))):
-            copy = pltpu.make_async_copy(src.at[part], dst.at[part], sems.at[2 * q + m])
+        part = pl.ds(8 * q, 8)
+        for m, (src, dst) in enumerate(((vo_ref, vo_hbm), (io_ref, io_hbm))):
+            copy = pltpu.make_async_copy(src.at[part], dst.at[part], sems.at[m, q])
             copy.start()
             copies.append(copy)
     for copy in copies:
@@ -296,21 +356,40 @@
     packed = pltpu.VMEM((4096, 256), B16)
     outside = pl.BlockSpec(memory_space=pltpu.HBM)
     inside = pl.BlockSpec(memory_space=pltpu.VMEM)
-    volts, amps, ends, induced = call(
+    return call(
         line_kernel,
-        (shape(4096, 128), shape(4096, 128), shape(3, 32, 128), shape(128, 128)),
+        (shape(4096, 128), shape(4096, 128), shape(4096, 256, dtype=B16), shape(256, 128, dtype=I32),
+         shape(3, 32, 128), shape(128, 128)),
         voltage, current, inductance, capacitance, drive, lengths,
         name="lines",
         in_specs=[outside] * 4 + [inside] * 2,
-        out_specs=(outside, outside, inside, inside),
+        out_specs=(outside, outside, outside, inside, inside, inside),
         scratch=[big, big, big, flat, flat, packed, packed, pltpu.VMEM((256, 128), F),
-                 pltpu.VMEM((256, 128), I32), pltpu.VMEM((128, 128), F), big, big,
+                 pltpu.VMEM((128, 128), F), big, big,
                  pltpu.VMEM((32, 32, 128), F), pltpu.VMEM((32, 32, 128), F),
-                 pltpu.SemaphoreType.DMA((8,)), pltpu.SemaphoreType.DMA((10,))],
+                 pltpu.SemaphoreType.DMA((3,)), pltpu.SemaphoreType.DMA((10,))],
         limit=53,
-        micros=18,
-    )
-    return volts.reshape(32, 128, 128), amps.reshape(32, 128, 128), ends, induced
+        micros=16,
+    )
+
+
+def last_voltages(volts, amps, capacitance, ends_at, fix):
+    big = pltpu.VMEM((32, 128, 128), F)
+    flat = pltpu.VMEM((4096, 128), F)
+    outside = pl.BlockSpec(memory_space=pltpu.HBM)
+    inside = pl.BlockSpec(memory_space=pltpu.VMEM)
+    return call(
+        last_kernel,
+        (shape(32, 128, 128), shape(32, 128, 128)),
+        volts, amps, capacitance, ends_at, fix,
+        name="last_voltages",
+        in_specs=[outside] * 3 + [inside] * 2,
+        out_specs=(outside, outside),
+        scratch=[big, big, flat, flat, pltpu.VMEM((4096, 256), B16), big, big,
+                 pltpu.SemaphoreType.DMA((2, 4)), pltpu.SemaphoreType.DMA((3, 4))],
+        limit=53,
+        micros=6,
+    )
 
 
 def junction_kernel(ends_ref, link_ref, a_ref, b_ref, ind_ref, fix_ref, indo_ref, buf):
@@ -356,31 +435,6 @@
         scratch=[pltpu.VMEM((32, 128), F)],
         limit=3,
         micros=1,
-    )
-
-
-def finish_kernel(v_ref, i_ref, fix_ref, vo_ref, io_ref):
-    sub8 = iota((8, 128), 0)
-    for c in range(32):
-        fix = [fix_ref[m, c : c + 1, :] for m in range(5)]
-        first, second = sub8 == 0, sub8 == 1
-        vo_ref[c] = v_ref[c] + jnp.where(first, fix[0], jnp.where(second, fix[1], jnp.where(sub8 == 2, fix[2], 0.0)))
-        io_ref[c] = i_ref[c] + jnp.where(first, fix[3], jnp.where(second, fix[4], 0.0))
-
-
-def finish(volts, amps, fix):
-    head = pl.BlockSpec((32, 8, 128), lambda n: (0, 0, 0))
-    return call(
-        finish_kernel,
-        (shape(32, 128, 128), shape(32, 128, 128)),
-        volts, amps, fix,
-        name="finish",
-        grid=(1,),
-        in_specs=[head, head, pl.BlockSpec((5, 32, 128), lambda n: (0, 0, 0))],
-        out_specs=(head, head),
-        aliases={0: 0, 1: 1},
-        limit=8,
-        micros=2,
     )
 
 
@@ -556,7 +610,7 @@
 
 def electric_kernel(
     e_hbm, h_hbm, below_ref, sigma_hbm, ind_ref, tan_ref, cell_s, perm_s, pos_hbm,
-    eo_hbm, val_s, plane_s, eo_ref, e_ref, h_ref, sigma_ref, pos_ref, sems, in_sems,
+    eo_hbm, val_s, plane_s, plane_t, eo_ref, e_ref, h_ref, sigma_ref, pos_ref, sems, in_sems,
 ):
     def fetch(x):
         return (
@@ -571,23 +625,25 @@
             copy.start()
     for k in range(3):
         val_s[k] = (tan_ref[k] * ind_ref[...]).T
-    for n in range(16):
-        rows = slice(8 * n, 8 * n + 8)
-        perm = perm_s[rows, :]
-        cell = cell_s[rows, :]
-        val = [take(val_s[k, rows, :], perm, 1) for k in range(3)]
+    for start in range(0, 16, 8):
+        spans = [slice(8 * n, 8 * n + 8) for n in range(start, start + 8)]
+        cells = [cell_s[rows, :] for rows in spans]
+        val = [[take(val_s[k, rows, :], perm_s[rows, :], 1) for k in range(3)] for rows in spans]
         for gap in (1, 2, 4, 8, 16, 32):
-            same = pltpu.roll(cell, gap, 1) == cell
-            val = [v + jnp.where(same, pltpu.roll(v, gap, 1), 0.0) for v in val]
-        for k in range(3):
-            val_s[k, rows, :] = val[k]
+            same = [pltpu.roll(cell, gap, 1) == cell for cell in cells]
+            moved = [[pltpu.roll(v, gap, 1) for v in row] for row in val]
+            val = [
+                [v + jnp.where(hit, w, 0.0) for v, w in zip(row, shifted)]
+                for row, shifted, hit in zip(val, moved, same)
+            ]
+        for rows, row in zip(spans, val):
+            for k in range(3):
+                val_s[k, rows, :] = row[k]
 
     sub = iota((8, 256), 0)
     lane = iota((8, 256), 1)
 
-    def one_layer(x, carry):
-        px = jnp.maximum(x - 1, 0)
-        first = x == 0
+    def spread_layer(x, plane_s):
         for h in range(2):
             tiles = [[], [], []]
             for n in range(16):
@@ -598,6 +654,10 @@
                     tiles[k].append(jnp.where(pos >= 0, picked, 0.0))
             for k in range(3):
                 plane_s[k, :, 128 * h : 128 * h + 128] = jnp.concatenate(tiles[k], 0).T
+
+    def update_layer(x, plane_s):
+        px = jnp.maximum(x - 1, 0)
+        first = x == 0
         for yb in range(16):
             rows = slice(8 * yb, 8 * yb + 8)
             m = [h_ref[k, x, rows, :] for k in range(3)]
@@ -622,16 +682,33 @@
             push = COURANT * inverse
             for k in range(3):
                 eo_ref[k, x, rows, :] = keep * e_ref[k, x, rows, :] + push * (curl[k] - plane_s[k, rows, :])
+        pltpu.make_async_copy(eo_ref.at[:, x], eo_hbm.at[:, x], sems.at[x]).start()
+
+    def arrive(x, which):
+        for copy in fetch(x)[which]:
+            copy.wait()
+
+    early, late = slice(0, 1), slice(1, 4)
+    arrive(0, early)
+    spread_layer(0, plane_s)
+
+    def two_layers(n, carry):
+        x = 2 * n
+        arrive(x + 1, early)
+        arrive(x, late)
+        spread_layer(x + 1, plane_t)
+        update_layer(x, plane_s)
+
+        @pl.when(n < 3)
+        def _():
+            arrive(x + 2, early)
+
+        arrive(x + 1, late)
+        spread_layer(jnp.minimum(x + 2, 7), plane_s)
+        update_layer(x + 1, plane_t)
         return carry
 
-    def send_layer(x, carry):
-        for copy in fetch(x):
-            copy.wait()
-        one_layer(x, carry)
-        pltpu.make_async_copy(eo_ref.at[:, x], eo_hbm.at[:, x], sems.at[x]).start()
-        return carry
-
-    lax.fori_loop(0, 8, send_layer, 0)
+    lax.fori_loop(0, 4, two_layers, 0)
     for x in range(8):
         pltpu.make_async_copy(eo_ref.at[:, x], eo_hbm.at[:, x], sems.at[x]).wait()
 
@@ -650,6 +727,7 @@
         scratch=[
             pltpu.VMEM((3, 128, 128), F),
             pltpu.VMEM((3, 128, 256), F),
+            pltpu.VMEM((3, 128, 256), F),
             whole, whole, whole,
             pltpu.VMEM((8, 128, 256), F),
             pltpu.VMEM((2, 8, 128, 128), I32),
@@ -690,7 +768,7 @@
     magnetic_new, layer = magnetics(electric, magnetic, above)
     drive, layer = lax.optimization_barrier((drive, layer))
     below = along(layer, BOTH, 1)
-    volts, amps, ends, induced = lines(
+    *state, ends, induced = lines(
         voltage, current, inverse_inductance, inverse_capacitance, drive, tube_length.reshape(1, 128)
     )
     ends, cells = lax.optimization_barrier((ends, cells))
@@ -701,7 +779,7 @@
     )
     induced, found = lax.optimization_barrier((induced, found))
     induced_local = exchange(induced)
-    volts, amps = finish(volts, amps, fix)
+    volts, amps = last_voltages(*state, fix)
     electric_new = electrics(electric, magnetic_new, below, conductivity, induced_local, steer, found)
     return electric_new, magnetic_new, volts, amps
 

time: 84 us -> 79.5 us (0.946)
  waiting for transfers between devices: 13.2 us -> 8.48 us
    all_to_all x2, waiting for transfers between devices: 13.2 us -> 8.47 us  [exchange(): return lax.all_to_all(x, BOTH, split_axis=0, concat_axis=0, tiled=True)]
  transfers between devices with their start and end apart: 5 -> 5, of which waited for: 2 -> 2; matrix products, arithmetic and copies ran while one was open for 0% -> 0% of each run, Pallas kernels for 40% -> 42%
where the time goes in v2:
time: 79.5 us; the launch traced here: 79.3 us
  Pallas kernels  44.9 us (56%)
  starting transfers between devices  24.9 us (31%)
  waiting for transfers between devices  8.48 us (11%)
  between operations  0.97 us (1%)
    pallas_call x7, Pallas kernels, call(): pl.pallas_call(body, out_shape=out, grid=grid, scratch_shapes=list(scratc...  44.9 us
    all_to_all x2, starting transfers between devices, exchange(): return lax.all_to_all(x, BOTH, split_axis=0, concat_axis=0, tiled=True)  16.6 us
    all_to_all x2, waiting for transfers between devices, exchange(): return lax.all_to_all(x, BOTH, split_axis=0, concat_axis=0, tiled=True)  8.47 us
    ppermute x2, starting transfers between devices, along(): lax.ppermute(x, axis, [(i, i + by) for i in range(peers) if 0 <= i + by <...  8.28 us
  transfers between devices with their start and end apart: 5, of which 2 were waited for; matrix products, arithmetic and copies ran while one was open for 0% of the time, Pallas kernels for 42%

profile of v2, /device:TPU:1, one launch (start us, length us, event | category | flops | bytes accessed | tf_op | source)
XLA Modules:
  0.0 79.3 jit_solution(18148564237881242748)
XLA Ops:
  0.6 4.3 %samples.1 = (f32[128,128]{1,0:T(8,128)}, f32[2,128,256]{2,1,0:T(8,128)}) custom-call(f32[3,8,128,256]{3,2,1,0:T(8,128)} %e_hbm.5, s32[128,128]{1,0:T(8,128)} %bitcast.16, f32[3,128,128]{2,1,0:T(8,128)} %bitcast.12), custom_call_target="tpu_custom_call" | custom-call | bytes 14760000 | tf_op jit(solution)/shard_map/samples/pallas_call | solution.py:30
  4.9 6.0 %collective-permute-start = (f32[2,128,256]{2,1,0:T(8,128)}, f32[2,128,256]{2,1,0:T(8,128)S(1)}, u32[]{:S(2)}, u32[]{:S(2)}) collective-permute-start(f32[2,128,256]{2,1,0:T(8,128)} %get-tuple-element.29), channel_id=1, source_target_pairs={{1,0},{2,1},{3,2},{4,3},{5,4},{6,5},{7,6},{8,7},{9,8},{10,9},{11,1... | collective-permute-start | bytes 786440 | tf_op jit(solution)/shard_map/ppermute | solution.py:747
  10.9 7.9 %all-to-all-start = ((f32[128,1,128]{2,1,0:T(1,128)}), f32[128,1,128]{2,1,0:T(1,128)S(1)}, u32[]{:S(2)}, u32[]{:S(2)}) async-start(f32[128,1,128]{2,1,0:T(1,128)} %bitcast.20), calls=%async_computation | async-start | bytes 131072 | tf_op jit(solution)/shard_map/all_to_all | solution.py:756
  18.9 0.0 copy-start
  18.9 0.0 copy-start.5
  18.9 0.0 collective-permute-done.above_ref
  18.9 4.6 %magnetics.1 = (f32[3,8,128,256]{3,2,1,0:T(8,128)}, f32[2,128,256]{2,1,0:T(8,128)S(1)}) custom-call(f32[3,8,128,256]{3,2,1,0:T(8,128)} %e_hbm.5, f32[3,8,128,256]{3,2,1,0:T(8,128)} %h_hbm.1, f32[2,128,256]{2,1,0:T(8,128)S(1)} %collective-permute-done.above_ref), custom_call_target="tpu_custom_call" | custom-call | bytes 14760000 | tf_op jit(solution)/shard_map/magnetics/pallas_call | solution.py:30
  23.6 5.2 %all-to-all-done = f32[128,1,128]{2,1,0:T(1,128)S(1)} async-done(((f32[128,1,128]{2,1,0:T(1,128)}), f32[128,1,128]{2,1,0:T(1,128)S(1)}, u32[]{:S(2)}, u32[]{:S(2)}) %all-to-all-start) | async-done | bytes 65568 | tf_op jit(solution)/shard_map/all_to_all | solution.py:756
  28.7 2.2 %collective-permute-start.1 = (f32[2,128,256]{2,1,0:T(8,128)S(1)}, f32[2,128,256]{2,1,0:T(8,128)S(1)}, u32[]{:S(2)}, u32[]{:S(2)}) collective-permute-start(f32[2,128,256]{2,1,0:T(8,128)S(1)} %get-tuple-element.33), channel_id=1, source_target_pairs={{0,1},{1,2},{2,3},{3,4},{4,5},{5,6},{6,7},{7,8},{8,9},{9,10},{10,1... | collective-permute-start | bytes 786440 | tf_op jit(solution)/shard_map/ppermute | solution.py:747
  31.0 0.0 copy-done
  31.0 0.0 copy-done.5
  31.0 0.0 copy-start.4
  31.0 0.0 copy-start.1
  31.0 0.0 copy-start.6
  31.0 15.1 %lines.1 = (f32[4096,128]{1,0:T(8,128)}, f32[4096,128]{1,0:T(8,128)}, bf16[4096,256]{1,0:T(8,128)(2,1)}, s32[256,128]{1,0:T(8,128)S(1)}, f32[3,32,128]{2,1,0:T(8,128)S(1)}, /*index=5*/f32[128,128]{1,0:T(8,128)S(1)}) custom-call(f32[32,128,128]{2,1,0:T(8,128)} %v_hbm.1, f32[32,128,128]{2,1,0:T(8,128)} %i_hbm.1, f32[32,32,128]{2,1,0:T(8,128)S(1)} %copy-done, ...), custom_call_target="tpu_custom_call" | custom-call | bytes 59040000 | tf_op jit(solution)/shard_map/lines/pallas_call | solution.py:30
  46.1 0.1 collective-permute-start.2
  46.2 0.0 copy-done.4
  46.2 6.1 %search.1 = (s32[128,128]{1,0:T(8,128)S(1)}, s32[128,128]{1,0:T(8,128)S(1)}, s32[2,8,128,128]{3,2,1,0:T(8,128)S(1)}) custom-call(s32[128,128]{1,0:T(8,128)S(1)} %bitcast.17), custom_call_target="tpu_custom_call" | custom-call | bytes 14760000 | tf_op jit(solution)/shard_map/search/pallas_call | solution.py:30
  52.3 0.0 copy-start.2
  52.3 0.0 collective-permute-done.2.ends_ref
  52.3 0.0 copy-done.1
  52.3 0.0 copy-done.6
  52.3 1.1 %junctions.1 = (f32[5,32,128]{2,1,0:T(8,128)S(1)}, f32[128,128]{1,0:T(8,128)}) custom-call(f32[3,32,128]{2,1,0:T(8,128)S(1)} %collective-permute-done.2.ends_ref, s32[1,128]{1,0:T(1,128)S(1)} %bitcast.19, f32[32,32,128]{2,1,0:T(8,128)S(1)} %copy-done, f32[32,32,128]{2,1,0:T(8,128)S(1)} %copy-done.1, f32[128,128]{1,0:T(8,128)S(1)} %get-tuple-element.37.ind_ref), custom_call_target="tpu_custom_call" | custom-call | bytes 3690000 | tf_op jit(solution)/shard_map/junctions/pallas_call | solution.py:30
  53.4 0.0 copy-done.2
  53.4 8.6 %all-to-all-start.1 = ((f32[128,1,128]{2,1,0:T(1,128)}), f32[128,1,128]{2,1,0:T(1,128)S(1)}, u32[]{:S(2)}, u32[]{:S(2)}) async-start(f32[128,1,128]{2,1,0:T(1,128)} %bitcast.8), calls=%async_computation.1 | async-start | bytes 131072 | tf_op jit(solution)/shard_map/all_to_all | solution.py:756
  62.0 0.0 copy-start.3
  62.0 6.6 %last_voltages.1 = (f32[32,128,128]{2,1,0:T(8,128)}, f32[32,128,128]{2,1,0:T(8,128)}) custom-call(f32[4096,128]{1,0:T(8,128)} %get-tuple-element.47.v_hbm, f32[4096,128]{1,0:T(8,128)} %get-tuple-element.48.i_hbm, bf16[4096,256]{1,0:T(8,128)(2,1)} %get-tuple-element.49.b_hbm, s32[256,128]{1,0:T(8,128)S(1)} %get-tuple-element.50.eg, ...), custom_call_target="tpu_custom_call" | custom-call | bytes 22140000 | tf_op jit(solution)/shard_map/last_voltages/pallas_call | solution.py:30
  68.6 3.3 %all-to-all-done.1 = f32[128,1,128]{2,1,0:T(1,128)S(1)} async-done(((f32[128,1,128]{2,1,0:T(1,128)}), f32[128,1,128]{2,1,0:T(1,128)S(1)}, u32[]{:S(2)}, u32[]{:S(2)}) %all-to-all-start.1) | async-done | bytes 65568 | tf_op jit(solution)/shard_map/all_to_all | solution.py:756
  71.9 0.0 collective-permute-done.1.below_ref
  71.9 0.0 copy-done.3
  71.9 7.2 %electrics.1 = f32[3,8,128,256]{3,2,1,0:T(8,128)} custom-call(f32[3,8,128,256]{3,2,1,0:T(8,128)} %e_hbm.5, f32[3,8,128,256]{3,2,1,0:T(8,128)} %get-tuple-element.26.h_hbm, f32[2,128,256]{2,1,0:T(8,128)S(1)} %collective-permute-done.1.below_ref, f32[8,128,256]{2,1,0:T(8,128)} %sigma_hbm.1, f32[128,128]{1,0:T(8,128)S(1)} %bitcast.14, ...), custom_call_target="tpu_custom_call" | custom-call | bytes 22140000 | tf_op jit(solution)/shard_map/electrics/pallas_call | solution.py:30
Async XLA Ops:
  4.9 14.0 %collective-permute-start = (f32[2,128,256]{2,1,0:T(8,128)}, f32[2,128,256]{2,1,0:T(8,128)S(1)}, u32[]{:S(2)}, u32[]{:S(2)}) collective-permute-start(f32[2,128,256]{2,1,0:T(8,128)} %get-tuple-element.29), channel_id=1, source_target_pairs={{1,0},{2,1},{3,2},{4,3},{5,4},{6,5},{7,6},{8,7},{9,8},{10,9},{11,1... | collective-permute-start | bytes 786440 | tf_op jit(solution)/shard_map/ppermute | solution.py:747
  10.9 17.8 %all-to-all-start = ((f32[128,1,128]{2,1,0:T(1,128)}), f32[128,1,128]{2,1,0:T(1,128)S(1)}, u32[]{:S(2)}, u32[]{:S(2)}) async-start(f32[128,1,128]{2,1,0:T(1,128)} %bitcast.20), calls=%async_computation | async-start | bytes 131072 | tf_op jit(solution)/shard_map/all_to_all | solution.py:756
  18.9 12.1 %copy-start = (f32[32,32,128]{2,1,0:T(8,128)S(1)}, f32[32,32,128]{2,1,0:T(8,128)}, u32[]{:S(2)}) copy-start(f32[32,32,128]{2,1,0:T(8,128)} %a_ref.1) | copy-start | bytes 1572868
  18.9 12.1 %copy-start.5 = (s32[128]{0:T(128)S(1)}, s32[128]{0:T(128)}, u32[]{:S(2)}) copy-start(s32[128]{0:T(128)} %param.20) | copy-start | bytes 1540
  28.7 43.2 %collective-permute-start.1 = (f32[2,128,256]{2,1,0:T(8,128)S(1)}, f32[2,128,256]{2,1,0:T(8,128)S(1)}, u32[]{:S(2)}, u32[]{:S(2)}) collective-permute-start(f32[2,128,256]{2,1,0:T(8,128)S(1)} %get-tuple-element.33), channel_id=1, source_target_pairs={{0,1},{1,2},{2,3},{3,4},{4,5},{5,6},{6,7},{7,8},{8,9},{9,10},{10,1... | collective-permute-start | bytes 786440 | tf_op jit(solution)/shard_map/ppermute | solution.py:747
  31.0 15.2 %copy-start.4 = (s32[1,16384]{1,0:T(1,128)S(1)}, s32[1,16384]{1,0:T(1,128)}, u32[]{:S(2)}) copy-start(s32[1,16384]{1,0:T(1,128)} %param.19) | copy-start | bytes 196612
  31.0 21.3 %copy-start.1 = (f32[32,32,128]{2,1,0:T(8,128)S(1)}, f32[32,32,128]{2,1,0:T(8,128)}, u32[]{:S(2)}) copy-start(f32[32,32,128]{2,1,0:T(8,128)} %b_ref.1) | copy-start | bytes 1572868
  31.0 21.3 %copy-start.6 = (s32[128]{0:T(128)S(1)}, s32[128]{0:T(128)}, u32[]{:S(2)}) copy-start(s32[128]{0:T(128)} %param.21) | copy-start | bytes 1540
  46.1 6.2 %collective-permute-start.2 = (f32[3,32,128]{2,1,0:T(8,128)S(1)}, f32[3,32,128]{2,1,0:T(8,128)S(1)}, u32[]{:S(2)}, u32[]{:S(2)}) collective-permute-start(f32[3,32,128]{2,1,0:T(8,128)S(1)} %get-tuple-element.36), channel_id=1, source_target_pairs={{0,1},{1,2},{2,3},{3,0},{4,5},{5,6},{6,7},{7,4},{8,9},{9,10},{10,1... | collective-permute-start | bytes 147464 | tf_op jit(solution)/shard_map/ppermute | solution.py:752
  52.3 1.1 %copy-start.2 = (s32[2,8,128,128]{3,2,1,0:T(8,128)}, s32[2,8,128,128]{3,2,1,0:T(8,128)S(1)}, u32[]{:S(2)}) copy-start(s32[2,8,128,128]{3,2,1,0:T(8,128)S(1)} %get-tuple-element.46.pos_hbm) | copy-start | bytes 3145732
  53.4 18.5 %all-to-all-start.1 = ((f32[128,1,128]{2,1,0:T(1,128)}), f32[128,1,128]{2,1,0:T(1,128)S(1)}, u32[]{:S(2)}, u32[]{:S(2)}) async-start(f32[128,1,128]{2,1,0:T(1,128)} %bitcast.8), calls=%async_computation.1 | async-start | bytes 131072 | tf_op jit(solution)/shard_map/all_to_all | solution.py:756
  62.0 9.9 %copy-start.3 = (f32[3,1,16384]{2,1,0:T(1,128)S(1)}, f32[3,1,16384]{2,1,0:T(1,128)}, u32[]{:S(2)}) copy-start(f32[3,1,16384]{2,1,0:T(1,128)} %param.18) | copy-start | bytes 589828

commit v3 on v2

--- a/solution.py
+++ b/solution.py
@@ -546,9 +546,8 @@
     return keys
 
 
-def search_kernel(idx_ref, cell_ref, perm_ref, pos_ref):
+def sort_cells(idx_ref, cell_ref, perm_ref):
     sub8 = iota((8, 128), 0)
-    lane8 = iota((8, 128), 1)
     keys = []
     for n in range(16):
         owner = sub8 + 8 * n
@@ -558,9 +557,13 @@
     cell_ref[...] = keys >> 7
     perm_ref[...] = keys & 127
 
+
+def find_cells(cell_ref, pos_ref, start):
+    lane8 = iota((8, 128), 1)
+
     def spread(n, carry):
         rows = pl.ds(pl.multiple_of(n * 8, 8), 8)
-        cell = cell_ref[rows, :]
+        cell = cell_ref[pl.ds(pl.multiple_of(start + n * 8, 8), 8), :]
         for h in range(2):
             fence = {
                 p: take(cell, jnp.full((8, 128), 64 * h + p, I32), 1)
@@ -594,27 +597,49 @@
                 pos_ref[h, x, rows, :] = jnp.where(cur == target, pos, -1)
         return carry
 
-    lax.fori_loop(0, 16, spread, 0)
+    lax.fori_loop(0, 8, spread, 0)
+
+
+def first_search_kernel(idx_ref, cell_ref, perm_ref, pos_ref):
+    sort_cells(idx_ref, cell_ref, perm_ref)
+    find_cells(cell_ref, pos_ref, 0)
+
+
+def second_search_kernel(cell_ref, pos_ref):
+    find_cells(cell_ref, pos_ref, 64)
+
+
+HALF = (2, 8, 64, 128)
+
+
+def first_search(cells):
+    return call(
+        first_search_kernel,
+        (shape(128, 128, dtype=I32), shape(128, 128, dtype=I32), shape(*HALF, dtype=I32)),
+        cells,
+        name="first_search",
+        limit=53,
+        micros=3,
+    )
+
+
+def second_search(cell):
+    return call(second_search_kernel, shape(*HALF, dtype=I32), cell, name="second_search", limit=53, micros=3)
 
 
 def search(cells):
-    return call(
-        search_kernel,
-        (shape(128, 128, dtype=I32), shape(128, 128, dtype=I32), shape(2, 8, 128, 128, dtype=I32)),
-        cells,
-        name="search",
-        limit=4,
-        micros=4,
-    )
+    cell, perm, pos = first_search(cells)
+    return cell, perm, pos, second_search(cell)
 
 
 def electric_kernel(
-    e_hbm, h_hbm, below_ref, sigma_hbm, ind_ref, tan_ref, cell_s, perm_s, pos_hbm,
+    e_hbm, h_hbm, below_ref, sigma_hbm, ind_ref, tan_ref, cell_s, perm_s, pos_a, pos_b,
     eo_hbm, val_s, plane_s, plane_t, eo_ref, e_ref, h_ref, sigma_ref, pos_ref, sems, in_sems,
 ):
     def fetch(x):
         return (
-            pltpu.make_async_copy(pos_hbm.at[:, x], pos_ref.at[:, x], in_sems.at[0, x]),
+            pltpu.make_async_copy(pos_a.at[:, x], pos_ref.at[0, :, x], in_sems.at[0, x]),
+            pltpu.make_async_copy(pos_b.at[:, x], pos_ref.at[1, :, x], in_sems.at[4, x]),
             pltpu.make_async_copy(h_hbm.at[:, x], h_ref.at[:, x], in_sems.at[1, x]),
             pltpu.make_async_copy(e_hbm.at[:, x], e_ref.at[:, x], in_sems.at[2, x]),
             pltpu.make_async_copy(sigma_hbm.at[x], sigma_ref.at[x], in_sems.at[3, x]),
@@ -647,7 +672,7 @@
         for h in range(2):
             tiles = [[], [], []]
             for n in range(16):
-                pos = pos_ref[h, x, 8 * n : 8 * n + 8, :]
+                pos = pos_ref[n // 8, h, x, 8 * (n % 8) : 8 * (n % 8) + 8, :]
                 spot = pos & 127
                 for k in range(3):
                     picked = take(val_s[k, 8 * n : 8 * n + 8, :], spot, 1)
@@ -688,7 +713,7 @@
         for copy in fetch(x)[which]:
             copy.wait()
 
-    early, late = slice(0, 1), slice(1, 4)
+    early, late = slice(0, 2), slice(2, 5)
     arrive(0, early)
     spread_layer(0, plane_s)
 
@@ -722,7 +747,7 @@
         shape(3, 8, 128, 256),
         electric, magnetic_new, below, conductivity, induced, tangent, *found,
         name="electrics",
-        in_specs=[outside, outside, inside, outside, inside, inside, inside, inside, outside],
+        in_specs=[outside, outside, inside, outside, inside, inside, inside, inside, outside, outside],
         out_specs=outside,
         scratch=[
             pltpu.VMEM((3, 128, 128), F),
@@ -730,9 +755,9 @@
             pltpu.VMEM((3, 128, 256), F),
             whole, whole, whole,
             pltpu.VMEM((8, 128, 256), F),
-            pltpu.VMEM((2, 8, 128, 128), I32),
+            pltpu.VMEM((2,) + HALF, I32),
             pltpu.SemaphoreType.DMA((8,)),
-            pltpu.SemaphoreType.DMA((4, 8)),
+            pltpu.SemaphoreType.DMA((5, 8)),
         ],
         limit=53,
         micros=6,
@@ -764,23 +789,25 @@
     steer = tangent.reshape(3, 128, 128)
     drive_local, layer = samples(electric, cells, steer)
     above = along(layer, BOTH, -1)
+    drive_local, cells = lax.optimization_barrier((drive_local, cells))
     drive = exchange(drive_local)
+    cell, perm, pos_a = first_search(cells)
     magnetic_new, layer = magnetics(electric, magnetic, above)
-    drive, layer = lax.optimization_barrier((drive, layer))
+    drive, layer, cell, pos_a = lax.optimization_barrier((drive, layer, cell, pos_a))
     below = along(layer, BOTH, 1)
     *state, ends, induced = lines(
         voltage, current, inverse_inductance, inverse_capacitance, drive, tube_length.reshape(1, 128)
     )
-    ends, cells = lax.optimization_barrier((ends, cells))
+    ends, cell = lax.optimization_barrier((ends, cell))
     ends = around(ends, "cable")
-    found = search(cells)
+    pos_b = second_search(cell)
     fix, induced = junctions(
         ends, junction_link.reshape(1, 128), inverse_inductance, inverse_capacitance, induced
     )
-    induced, found = lax.optimization_barrier((induced, found))
+    induced, pos_b = lax.optimization_barrier((induced, pos_b))
     induced_local = exchange(induced)
     volts, amps = last_voltages(*state, fix)
-    electric_new = electrics(electric, magnetic_new, below, conductivity, induced_local, steer, found)
+    electric_new = electrics(electric, magnetic_new, below, conductivity, induced_local, steer, (cell, perm, pos_a, pos_b))
     return electric_new, magnetic_new, volts, amps
 
 

time: 79.5 us -> 78.8 us (level)
  waiting for transfers between devices: 8.48 us -> 4.43 us
  starting transfers between devices: 24.9 us -> 26.5 us
  local copies, waits for them, and re-layouts: 0.04 us -> 1.62 us
    all_to_all x2, waiting for transfers between devices: 8.47 us -> 4.43 us  [exchange(): return lax.all_to_all(x, BOTH, split_axis=0, concat_axis=0, tiled=True)]
    unnamed x14 -> x16, local copies, waits for them, and re-layouts: 0.04 us -> 1.62 us
    ppermute x1, starting transfers between devices: 0.09 us -> 1.2 us  [around(): return lax.ppermute(x, axis, [(i, (i + 1) % peers) for i in range(peers)])]
    pallas_call x7 -> x8, Pallas kernels: 44.9 us -> 45 us  [call(): pl.pallas_call(body, out_shape=out, grid=grid, scratch_shapes=list(scratc...]
  transfers between devices with their start and end apart: 5 -> 5, of which waited for: 2 -> 2; matrix products, arithmetic and copies ran while one was open for 0% -> 0% of each run, Pallas kernels for 42% -> 43%
where the time goes in v3:
time: 78.8 us; the launch traced here: 78.5 us
  Pallas kernels  45 us (57%)
  starting transfers between devices  26.5 us (34%)
  waiting for transfers between devices  4.43 us (6%)
  local copies, waits for them, and re-layouts  1.62 us (2%)
  between operations  0.95 us (1%)
    pallas_call x8, Pallas kernels, call(): pl.pallas_call(body, out_shape=out, grid=grid, scratch_shapes=list(scratc...  45 us
    all_to_all x2, starting transfers between devices, exchange(): return lax.all_to_all(x, BOTH, split_axis=0, concat_axis=0, tiled=True)  17 us
    ppermute x2, starting transfers between devices, along(): lax.ppermute(x, axis, [(i, i + by) for i in range(peers) if 0 <= i + by <...  8.28 us
    all_to_all x2, waiting for transfers between devices, exchange(): return lax.all_to_all(x, BOTH, split_axis=0, concat_axis=0, tiled=True)  4.43 us
    unnamed x16, local copies, waits for them, and re-layouts  1.62 us
  transfers between devices with their start and end apart: 5, of which 2 were waited for; matrix products, arithmetic and copies ran while one was open for 0% of the time, Pallas kernels for 43%

profile of v3, /device:TPU:1, one launch (start us, length us, event | category | flops | bytes accessed | tf_op | source)
XLA Modules:
  0.0 78.5 jit_solution(13284305285747563883)
XLA Ops:
  0.6 0.0 copy-start.5
  0.6 4.3 %samples.1 = (f32[128,128]{1,0:T(8,128)}, f32[2,128,256]{2,1,0:T(8,128)}) custom-call(f32[3,8,128,256]{3,2,1,0:T(8,128)} %e_hbm.5, s32[128,128]{1,0:T(8,128)} %bitcast.16, f32[3,128,128]{2,1,0:T(8,128)} %bitcast.12), custom_call_target="tpu_custom_call" | custom-call | bytes 14760000 | tf_op jit(solution)/shard_map/samples/pallas_call | solution.py:30
  4.9 6.0 %collective-permute-start = (f32[2,128,256]{2,1,0:T(8,128)}, f32[2,128,256]{2,1,0:T(8,128)S(1)}, u32[]{:S(2)}, u32[]{:S(2)}) collective-permute-start(f32[2,128,256]{2,1,0:T(8,128)} %get-tuple-element.31), channel_id=1, source_target_pairs={{1,0},{2,1},{3,2},{4,3},{5,4},{6,5},{7,6},{8,7},{9,8},{10,9},{11,1... | collective-permute-start | bytes 786440 | tf_op jit(solution)/shard_map/ppermute | solution.py:772
  11.0 7.9 %all-to-all-start = ((f32[128,1,128]{2,1,0:T(1,128)}), f32[128,1,128]{2,1,0:T(1,128)S(1)}, u32[]{:S(2)}, u32[]{:S(2)}) async-start(f32[128,1,128]{2,1,0:T(1,128)} %bitcast.20), calls=%async_computation | async-start | bytes 131072 | tf_op jit(solution)/shard_map/all_to_all | solution.py:781
  18.9 0.0 copy-done.5
  18.9 3.2 %first_search.1 = (s32[128,128]{1,0:T(8,128)S(1)}, s32[128,128]{1,0:T(8,128)S(1)}, s32[2,8,64,128]{3,2,1,0:T(8,128)S(1)}) custom-call(s32[128,128]{1,0:T(8,128)S(1)} %bitcast.17), custom_call_target="tpu_custom_call" | custom-call | bytes 11070000 | tf_op jit(solution)/shard_map/first_search/pallas_call | solution.py:30
  22.2 0.0 copy-start.4
  22.2 0.8 %copy-done.4 = s32[2,8,64,128]{3,2,1,0:T(8,128)} copy-done((s32[2,8,64,128]{3,2,1,0:T(8,128)}, s32[2,8,64,128]{3,2,1,0:T(8,128)S(1)}, u32[]{:S(2)}) %copy-start.4) | copy-done | bytes 524312
  23.0 0.0 collective-permute-done.above_ref
  23.0 4.6 %magnetics.1 = (f32[3,8,128,256]{3,2,1,0:T(8,128)}, f32[2,128,256]{2,1,0:T(8,128)S(1)}) custom-call(f32[3,8,128,256]{3,2,1,0:T(8,128)} %e_hbm.5, f32[3,8,128,256]{3,2,1,0:T(8,128)} %h_hbm.1, f32[2,128,256]{2,1,0:T(8,128)S(1)} %collective-permute-done.above_ref), custom_call_target="tpu_custom_call" | custom-call | bytes 14760000 | tf_op jit(solution)/shard_map/magnetics/pallas_call | solution.py:30
  27.6 1.1 %all-to-all-done = f32[128,1,128]{2,1,0:T(1,128)S(1)} async-done(((f32[128,1,128]{2,1,0:T(1,128)}), f32[128,1,128]{2,1,0:T(1,128)S(1)}, u32[]{:S(2)}, u32[]{:S(2)}) %all-to-all-start) | async-done | bytes 65568 | tf_op jit(solution)/shard_map/all_to_all | solution.py:781
  28.7 2.2 %collective-permute-start.1 = (f32[2,128,256]{2,1,0:T(8,128)S(1)}, f32[2,128,256]{2,1,0:T(8,128)S(1)}, u32[]{:S(2)}, u32[]{:S(2)}) collective-permute-start(f32[2,128,256]{2,1,0:T(8,128)S(1)} %get-tuple-element.39), channel_id=1, source_target_pairs={{0,1},{1,2},{2,3},{3,4},{4,5},{5,6},{6,7},{7,8},{8,9},{9,10},{10,1... | collective-permute-start | bytes 786440 | tf_op jit(solution)/shard_map/ppermute | solution.py:772
  31.0 0.0 copy-done.1
  31.0 0.0 copy-done.6
  31.0 0.0 copy-start.2
  31.0 0.0 copy-start.7
  31.0 15.0 %lines.1 = (f32[4096,128]{1,0:T(8,128)}, f32[4096,128]{1,0:T(8,128)}, bf16[4096,256]{1,0:T(8,128)(2,1)}, s32[256,128]{1,0:T(8,128)S(1)}, f32[3,32,128]{2,1,0:T(8,128)S(1)}, /*index=5*/f32[128,128]{1,0:T(8,128)S(1)}) custom-call(f32[32,128,128]{2,1,0:T(8,128)} %v_hbm.1, f32[32,128,128]{2,1,0:T(8,128)} %i_hbm.1, f32[32,32,128]{2,1,0:T(8,128)S(1)} %copy-done.1, ...), custom_call_target="tpu_custom_call" | custom-call | bytes 59040000 | tf_op jit(solution)/shard_map/lines/pallas_call | solution.py:30
  46.1 1.2 %collective-permute-start.2 = (f32[3,32,128]{2,1,0:T(8,128)S(1)}, f32[3,32,128]{2,1,0:T(8,128)S(1)}, u32[]{:S(2)}, u32[]{:S(2)}) collective-permute-start(f32[3,32,128]{2,1,0:T(8,128)S(1)} %get-tuple-element.43), channel_id=1, source_target_pairs={{0,1},{1,2},{2,3},{3,0},{4,5},{5,6},{6,7},{7,4},{8,9},{9,10},{10,1... | collective-permute-start | bytes 147464 | tf_op jit(solution)/shard_map/ppermute | solution.py:777
  47.3 2.8 %second_search.1.pos_b = s32[2,8,64,128]{3,2,1,0:T(8,128)S(1)} custom-call(s32[128,128]{1,0:T(8,128)S(1)} %get-tuple-element.46.cell_ref.cell_s), custom_call_target="tpu_custom_call" | custom-call | bytes 11070000 | tf_op jit(solution)/shard_map/second_search/pallas_call | solution.py:30
  50.1 0.0 copy-start
  50.2 0.8 %copy-done = s32[2,8,64,128]{3,2,1,0:T(8,128)} copy-done((s32[2,8,64,128]{3,2,1,0:T(8,128)}, s32[2,8,64,128]{3,2,1,0:T(8,128)S(1)}, u32[]{:S(2)}) %copy-start) | copy-done | bytes 524312
  50.9 0.0 collective-permute-done.2.ends_ref
  51.0 0.0 copy-done.2
  51.0 0.0 copy-done.7
  51.0 1.1 %junctions.1 = (f32[5,32,128]{2,1,0:T(8,128)S(1)}, f32[128,128]{1,0:T(8,128)}) custom-call(f32[3,32,128]{2,1,0:T(8,128)S(1)} %collective-permute-done.2.ends_ref, s32[1,128]{1,0:T(1,128)S(1)} %bitcast.19, f32[32,32,128]{2,1,0:T(8,128)S(1)} %copy-done.1, f32[32,32,128]{2,1,0:T(8,128)S(1)} %copy-done.2, f32[128,128]{1,0:T(8,128)S(1)} %get-tuple-element.44.ind_ref), custom_call_target="tpu_custom_call" | custom-call | bytes 3690000 | tf_op jit(solution)/shard_map/junctions/pallas_call | solution.py:30
  52.0 9.1 %all-to-all-start.1 = ((f32[128,1,128]{2,1,0:T(1,128)}), f32[128,1,128]{2,1,0:T(1,128)S(1)}, u32[]{:S(2)}, u32[]{:S(2)}) async-start(f32[128,1,128]{2,1,0:T(1,128)} %bitcast.8), calls=%async_computation.1 | async-start | bytes 131072 | tf_op jit(solution)/shard_map/all_to_all | solution.py:781
  61.2 0.0 copy-start.3
  61.2 6.6 %last_voltages.1 = (f32[32,128,128]{2,1,0:T(8,128)}, f32[32,128,128]{2,1,0:T(8,128)}) custom-call(f32[4096,128]{1,0:T(8,128)} %get-tuple-element.51.v_hbm, f32[4096,128]{1,0:T(8,128)} %get-tuple-element.52.i_hbm, bf16[4096,256]{1,0:T(8,128)(2,1)} %get-tuple-element.53.b_hbm, s32[256,128]{1,0:T(8,128)S(1)} %get-tuple-element.54.eg, ...), custom_call_target="tpu_custom_call" | custom-call | bytes 22140000 | tf_op jit(solution)/shard_map/last_voltages/pallas_call | solution.py:30
  67.7 3.3 %all-to-all-done.1 = f32[128,1,128]{2,1,0:T(1,128)S(1)} async-done(((f32[128,1,128]{2,1,0:T(1,128)}), f32[128,1,128]{2,1,0:T(1,128)S(1)}, u32[]{:S(2)}, u32[]{:S(2)}) %all-to-all-start.1) | async-done | bytes 65568 | tf_op jit(solution)/shard_map/all_to_all | solution.py:781
  71.0 0.0 collective-permute-done.1.below_ref
  71.0 0.0 copy-done.3
  71.0 7.4 %electrics.1 = f32[3,8,128,256]{3,2,1,0:T(8,128)} custom-call(f32[3,8,128,256]{3,2,1,0:T(8,128)} %e_hbm.5, f32[3,8,128,256]{3,2,1,0:T(8,128)} %get-tuple-element.28.h_hbm, f32[2,128,256]{2,1,0:T(8,128)S(1)} %collective-permute-done.1.below_ref, f32[8,128,256]{2,1,0:T(8,128)} %sigma_hbm.1, f32[128,128]{1,0:T(8,128)S(1)} %bitcast.15, ...), custom_call_target="tpu_custom_call" | custom-call | bytes 22140000 | tf_op jit(solution)/shard_map/electrics/pallas_call | solution.py:30
  (2 shorter events, 0.0 us)
Async XLA Ops:
  0.6 18.3 %copy-start.5 = (s32[1,16384]{1,0:T(1,128)S(1)}, s32[1,16384]{1,0:T(1,128)}, u32[]{:S(2)}) copy-start(s32[1,16384]{1,0:T(1,128)} %param.19) | copy-start | bytes 196612
  4.9 18.0 %collective-permute-start = (f32[2,128,256]{2,1,0:T(8,128)}, f32[2,128,256]{2,1,0:T(8,128)S(1)}, u32[]{:S(2)}, u32[]{:S(2)}) collective-permute-start(f32[2,128,256]{2,1,0:T(8,128)} %get-tuple-element.31), channel_id=1, source_target_pairs={{1,0},{2,1},{3,2},{4,3},{5,4},{6,5},{7,6},{8,7},{9,8},{10,9},{11,1... | collective-permute-start | bytes 786440 | tf_op jit(solution)/shard_map/ppermute | solution.py:772
  11.0 17.8 %all-to-all-start = ((f32[128,1,128]{2,1,0:T(1,128)}), f32[128,1,128]{2,1,0:T(1,128)S(1)}, u32[]{:S(2)}, u32[]{:S(2)}) async-start(f32[128,1,128]{2,1,0:T(1,128)} %bitcast.20), calls=%async_computation | async-start | bytes 131072 | tf_op jit(solution)/shard_map/all_to_all | solution.py:781
  22.2 0.8 %copy-start.4 = (s32[2,8,64,128]{3,2,1,0:T(8,128)}, s32[2,8,64,128]{3,2,1,0:T(8,128)S(1)}, u32[]{:S(2)}) copy-start(s32[2,8,64,128]{3,2,1,0:T(8,128)S(1)} %get-tuple-element.49.pos_a) | copy-start | bytes 1572868
  23.0 8.0 %copy-start.1 = (f32[32,32,128]{2,1,0:T(8,128)S(1)}, f32[32,32,128]{2,1,0:T(8,128)}, u32[]{:S(2)}) copy-start(f32[32,32,128]{2,1,0:T(8,128)} %a_ref.1) | copy-start | bytes 1572868
  23.0 8.0 %copy-start.6 = (s32[128]{0:T(128)S(1)}, s32[128]{0:T(128)}, u32[]{:S(2)}) copy-start(s32[128]{0:T(128)} %param.20) | copy-start | bytes 1540
  28.7 42.3 %collective-permute-start.1 = (f32[2,128,256]{2,1,0:T(8,128)S(1)}, f32[2,128,256]{2,1,0:T(8,128)S(1)}, u32[]{:S(2)}, u32[]{:S(2)}) collective-permute-start(f32[2,128,256]{2,1,0:T(8,128)S(1)} %get-tuple-element.39), channel_id=1, source_target_pairs={{0,1},{1,2},{2,3},{3,4},{4,5},{5,6},{6,7},{7,8},{8,9},{9,10},{10,1... | collective-permute-start | bytes 786440 | tf_op jit(solution)/shard_map/ppermute | solution.py:772
  31.0 19.9 %copy-start.2 = (f32[32,32,128]{2,1,0:T(8,128)S(1)}, f32[32,32,128]{2,1,0:T(8,128)}, u32[]{:S(2)}) copy-start(f32[32,32,128]{2,1,0:T(8,128)} %b_ref.1) | copy-start | bytes 1572868
  31.0 19.9 %copy-start.7 = (s32[128]{0:T(128)S(1)}, s32[128]{0:T(128)}, u32[]{:S(2)}) copy-start(s32[128]{0:T(128)} %param.21) | copy-start | bytes 1540
  46.1 4.9 %collective-permute-start.2 = (f32[3,32,128]{2,1,0:T(8,128)S(1)}, f32[3,32,128]{2,1,0:T(8,128)S(1)}, u32[]{:S(2)}, u32[]{:S(2)}) collective-permute-start(f32[3,32,128]{2,1,0:T(8,128)S(1)} %get-tuple-element.43), channel_id=1, source_target_pairs={{0,1},{1,2},{2,3},{3,0},{4,5},{5,6},{6,7},{7,4},{8,9},{9,10},{10,1... | collective-permute-start | bytes 147464 | tf_op jit(solution)/shard_map/ppermute | solution.py:777
  50.1 0.8 %copy-start = (s32[2,8,64,128]{3,2,1,0:T(8,128)}, s32[2,8,64,128]{3,2,1,0:T(8,128)S(1)}, u32[]{:S(2)}) copy-start(s32[2,8,64,128]{3,2,1,0:T(8,128)S(1)} %second_search.1.pos_b) | copy-start | bytes 1572868
  52.0 19.0 %all-to-all-start.1 = ((f32[128,1,128]{2,1,0:T(1,128)}), f32[128,1,128]{2,1,0:T(1,128)S(1)}, u32[]{:S(2)}, u32[]{:S(2)}) async-start(f32[128,1,128]{2,1,0:T(1,128)} %bitcast.8), calls=%async_computation.1 | async-start | bytes 131072 | tf_op jit(solution)/shard_map/all_to_all | solution.py:781
  61.2 9.9 %copy-start.3 = (f32[3,1,16384]{2,1,0:T(1,128)S(1)}, f32[3,1,16384]{2,1,0:T(1,128)}, u32[]{:S(2)}) copy-start(f32[3,1,16384]{2,1,0:T(1,128)} %param.18) | copy-start | bytes 589828

commit v4 on v3

--- a/solution.py
+++ b/solution.py
@@ -558,7 +558,7 @@
     perm_ref[...] = keys & 127
 
 
-def find_cells(cell_ref, pos_ref, start):
+def find_cells(cell_ref, pos_hbm, start, pos_ref, sems):
     lane8 = iota((8, 128), 1)
 
     def spread(n, carry):
@@ -597,34 +597,53 @@
                 pos_ref[h, x, rows, :] = jnp.where(cur == target, pos, -1)
         return carry
 
-    lax.fori_loop(0, 8, spread, 0)
-
-
-def first_search_kernel(idx_ref, cell_ref, perm_ref, pos_ref):
+    copies = []
+    for part in range(4):
+        lax.fori_loop(2 * part, 2 * part + 2, spread, 0)
+        rows = pl.ds(16 * part, 16)
+        copies.append(pltpu.make_async_copy(pos_ref.at[:, :, rows], pos_hbm.at[:, :, rows], sems.at[part]))
+        copies[part].start()
+    for copy in copies:
+        copy.wait()
+
+
+def first_search_kernel(idx_ref, cell_ref, perm_ref, pos_hbm, pos_ref, sems):
     sort_cells(idx_ref, cell_ref, perm_ref)
-    find_cells(cell_ref, pos_ref, 0)
-
-
-def second_search_kernel(cell_ref, pos_ref):
-    find_cells(cell_ref, pos_ref, 64)
+    find_cells(cell_ref, pos_hbm, 0, pos_ref, sems)
+
+
+def second_search_kernel(cell_ref, pos_hbm, pos_ref, sems):
+    find_cells(cell_ref, pos_hbm, 64, pos_ref, sems)
 
 
 HALF = (2, 8, 64, 128)
 
 
 def first_search(cells):
+    inside = pl.BlockSpec(memory_space=pltpu.VMEM)
     return call(
         first_search_kernel,
-        (shape(128, 128, dtype=I32), shape(128, 128, dtype=I32), shape(*HALF, dtype=I32)),
+        (shape(128, 128, dtype=I32), shape(128, 128, dtype=I32), pltpu.HBM(HALF, I32)),
         cells,
         name="first_search",
+        out_specs=(inside, inside, pl.BlockSpec(memory_space=pltpu.HBM)),
+        scratch=[pltpu.VMEM(HALF, I32), pltpu.SemaphoreType.DMA((4,))],
         limit=53,
         micros=3,
     )
 
 
 def second_search(cell):
-    return call(second_search_kernel, shape(*HALF, dtype=I32), cell, name="second_search", limit=53, micros=3)
+    return call(
+        second_search_kernel,
+        pltpu.HBM(HALF, I32),
+        cell,
+        name="second_search",
+        out_specs=pl.BlockSpec(memory_space=pltpu.HBM),
+        scratch=[pltpu.VMEM(HALF, I32), pltpu.SemaphoreType.DMA((4,))],
+        limit=53,
+        micros=3,
+    )
 
 
 def search(cells):

time: 78.8 us -> 78.6 us (level)
  local copies, waits for them, and re-layouts: 1.62 us -> 0.04 us
  Pallas kernels: 45 us -> 46.4 us
    unnamed x16 -> x12, local copies, waits for them, and re-layouts: 1.62 us -> 0.04 us
    pallas_call x8, Pallas kernels: 45 us -> 46.4 us  [call(): pl.pallas_call(body, out_shape=out, grid=grid, scratch_shapes=list(scratc...]
  transfers between devices with their start and end apart: 5 -> 5, of which waited for: 2 -> 2; matrix products, arithmetic and copies ran while one was open for 0% -> 0% of each run, Pallas kernels for 43% -> 44%
where the time goes in v4:
time: 78.6 us; the launch traced here: 78.4 us
  Pallas kernels  46.4 us (59%)
  starting transfers between devices  26.4 us (34%)
  waiting for transfers between devices  4.55 us (6%)
  between operations  0.98 us (1%)
    pallas_call x8, Pallas kernels, call(): pl.pallas_call(body, out_shape=out, grid=grid, scratch_shapes=list(scratc...  46.4 us
    all_to_all x2, starting transfers between devices, exchange(): return lax.all_to_all(x, BOTH, split_axis=0, concat_axis=0, tiled=True)  17 us
    ppermute x2, starting transfers between devices, along(): lax.ppermute(x, axis, [(i, i + by) for i in range(peers) if 0 <= i + by <...  8.28 us
    all_to_all x2, waiting for transfers between devices, exchange(): return lax.all_to_all(x, BOTH, split_axis=0, concat_axis=0, tiled=True)  4.55 us
  transfers between devices with their start and end apart: 5, of which 2 were waited for; matrix products, arithmetic and copies ran while one was open for 0% of the time, Pallas kernels for 44%

profile of v4, /device:TPU:1, one launch (start us, length us, event | category | flops | bytes accessed | tf_op | source)
XLA Modules:
  0.0 78.4 jit_solution(3368685495352690851)
XLA Ops:
  0.6 0.0 copy-start.3
  0.6 4.3 %samples.1 = (f32[128,128]{1,0:T(8,128)}, f32[2,128,256]{2,1,0:T(8,128)}) custom-call(f32[3,8,128,256]{3,2,1,0:T(8,128)} %e_hbm.5, s32[128,128]{1,0:T(8,128)} %bitcast.16, f32[3,128,128]{2,1,0:T(8,128)} %bitcast.12), custom_call_target="tpu_custom_call" | custom-call | bytes 14760000 | tf_op jit(solution)/shard_map/samples/pallas_call | solution.py:30
  4.9 6.0 %collective-permute-start = (f32[2,128,256]{2,1,0:T(8,128)}, f32[2,128,256]{2,1,0:T(8,128)S(1)}, u32[]{:S(2)}, u32[]{:S(2)}) collective-permute-start(f32[2,128,256]{2,1,0:T(8,128)} %get-tuple-element.31), channel_id=1, source_target_pairs={{1,0},{2,1},{3,2},{4,3},{5,4},{6,5},{7,6},{8,7},{9,8},{10,9},{11,1... | collective-permute-start | bytes 786440 | tf_op jit(solution)/shard_map/ppermute | solution.py:791
  11.0 7.9 %all-to-all-start = ((f32[128,1,128]{2,1,0:T(1,128)}), f32[128,1,128]{2,1,0:T(1,128)S(1)}, u32[]{:S(2)}, u32[]{:S(2)}) async-start(f32[128,1,128]{2,1,0:T(1,128)} %bitcast.20), calls=%async_computation | async-start | bytes 131072 | tf_op jit(solution)/shard_map/all_to_all | solution.py:800
  18.9 0.0 copy-done.3
  18.9 3.9 %first_search.1 = (s32[128,128]{1,0:T(8,128)S(1)}, s32[128,128]{1,0:T(8,128)S(1)}, s32[2,8,64,128]{3,2,1,0:T(8,128)}) custom-call(s32[128,128]{1,0:T(8,128)S(1)} %bitcast.17), custom_call_target="tpu_custom_call" | custom-call | bytes 11070000 | tf_op jit(solution)/shard_map/first_search/pallas_call | solution.py:30
  22.9 0.0 copy-start
  22.9 0.0 copy-start.4
  22.9 0.0 collective-permute-done.above_ref
  22.9 4.6 %magnetics.1 = (f32[3,8,128,256]{3,2,1,0:T(8,128)}, f32[2,128,256]{2,1,0:T(8,128)S(1)}) custom-call(f32[3,8,128,256]{3,2,1,0:T(8,128)} %e_hbm.5, f32[3,8,128,256]{3,2,1,0:T(8,128)} %h_hbm.1, f32[2,128,256]{2,1,0:T(8,128)S(1)} %collective-permute-done.above_ref), custom_call_target="tpu_custom_call" | custom-call | bytes 14760000 | tf_op jit(solution)/shard_map/magnetics/pallas_call | solution.py:30
  27.5 1.2 %all-to-all-done = f32[128,1,128]{2,1,0:T(1,128)S(1)} async-done(((f32[128,1,128]{2,1,0:T(1,128)}), f32[128,1,128]{2,1,0:T(1,128)S(1)}, u32[]{:S(2)}, u32[]{:S(2)}) %all-to-all-start) | async-done | bytes 65568 | tf_op jit(solution)/shard_map/all_to_all | solution.py:800
  28.7 2.2 %collective-permute-start.1 = (f32[2,128,256]{2,1,0:T(8,128)S(1)}, f32[2,128,256]{2,1,0:T(8,128)S(1)}, u32[]{:S(2)}, u32[]{:S(2)}) collective-permute-start(f32[2,128,256]{2,1,0:T(8,128)S(1)} %get-tuple-element.39), channel_id=1, source_target_pairs={{0,1},{1,2},{2,3},{3,4},{4,5},{5,6},{6,7},{7,8},{8,9},{9,10},{10,1... | collective-permute-start | bytes 786440 | tf_op jit(solution)/shard_map/ppermute | solution.py:791
  31.0 0.0 copy-done
  31.0 0.0 copy-done.4
  31.0 0.0 copy-start.1
  31.0 0.0 copy-start.5
  31.0 15.0 %lines.1 = (f32[4096,128]{1,0:T(8,128)}, f32[4096,128]{1,0:T(8,128)}, bf16[4096,256]{1,0:T(8,128)(2,1)}, s32[256,128]{1,0:T(8,128)S(1)}, f32[3,32,128]{2,1,0:T(8,128)S(1)}, /*index=5*/f32[128,128]{1,0:T(8,128)S(1)}) custom-call(f32[32,128,128]{2,1,0:T(8,128)} %v_hbm.1, f32[32,128,128]{2,1,0:T(8,128)} %i_hbm.1, f32[32,32,128]{2,1,0:T(8,128)S(1)} %copy-done, ...), custom_call_target="tpu_custom_call" | custom-call | bytes 59040000 | tf_op jit(solution)/shard_map/lines/pallas_call | solution.py:30
  46.1 1.1 %collective-permute-start.2 = (f32[3,32,128]{2,1,0:T(8,128)S(1)}, f32[3,32,128]{2,1,0:T(8,128)S(1)}, u32[]{:S(2)}, u32[]{:S(2)}) collective-permute-start(f32[3,32,128]{2,1,0:T(8,128)S(1)} %get-tuple-element.43), channel_id=1, source_target_pairs={{0,1},{1,2},{2,3},{3,0},{4,5},{5,6},{6,7},{7,4},{8,9},{9,10},{10,1... | collective-permute-start | bytes 147464 | tf_op jit(solution)/shard_map/ppermute | solution.py:796
  47.2 3.5 %second_search.1.pos_b = s32[2,8,64,128]{3,2,1,0:T(8,128)} custom-call(s32[128,128]{1,0:T(8,128)S(1)} %get-tuple-element.46.cell_ref.cell_s), custom_call_target="tpu_custom_call" | custom-call | bytes 11070000 | tf_op jit(solution)/shard_map/second_search/pallas_call | solution.py:30
  50.8 0.0 collective-permute-done.2.ends_ref
  50.8 0.0 copy-done.1
  50.8 0.0 copy-done.5
  50.8 1.1 %junctions.1 = (f32[5,32,128]{2,1,0:T(8,128)S(1)}, f32[128,128]{1,0:T(8,128)}) custom-call(f32[3,32,128]{2,1,0:T(8,128)S(1)} %collective-permute-done.2.ends_ref, s32[1,128]{1,0:T(1,128)S(1)} %bitcast.19, f32[32,32,128]{2,1,0:T(8,128)S(1)} %copy-done, f32[32,32,128]{2,1,0:T(8,128)S(1)} %copy-done.1, f32[128,128]{1,0:T(8,128)S(1)} %get-tuple-element.44.ind_ref), custom_call_target="tpu_custom_call" | custom-call | bytes 3690000 | tf_op jit(solution)/shard_map/junctions/pallas_call | solution.py:30
  51.9 9.1 %all-to-all-start.1 = ((f32[128,1,128]{2,1,0:T(1,128)}), f32[128,1,128]{2,1,0:T(1,128)S(1)}, u32[]{:S(2)}, u32[]{:S(2)}) async-start(f32[128,1,128]{2,1,0:T(1,128)} %bitcast.8), calls=%async_computation.1 | async-start | bytes 131072 | tf_op jit(solution)/shard_map/all_to_all | solution.py:800
  61.0 0.0 copy-start.2
  61.0 6.6 %last_voltages.1 = (f32[32,128,128]{2,1,0:T(8,128)}, f32[32,128,128]{2,1,0:T(8,128)}) custom-call(f32[4096,128]{1,0:T(8,128)} %get-tuple-element.51.v_hbm, f32[4096,128]{1,0:T(8,128)} %get-tuple-element.52.i_hbm, bf16[4096,256]{1,0:T(8,128)(2,1)} %get-tuple-element.53.b_hbm, s32[256,128]{1,0:T(8,128)S(1)} %get-tuple-element.54.eg, ...), custom_call_target="tpu_custom_call" | custom-call | bytes 22140000 | tf_op jit(solution)/shard_map/last_voltages/pallas_call | solution.py:30
  67.6 3.3 %all-to-all-done.1 = f32[128,1,128]{2,1,0:T(1,128)S(1)} async-done(((f32[128,1,128]{2,1,0:T(1,128)}), f32[128,1,128]{2,1,0:T(1,128)S(1)}, u32[]{:S(2)}, u32[]{:S(2)}) %all-to-all-start.1) | async-done | bytes 65568 | tf_op jit(solution)/shard_map/all_to_all | solution.py:800
  70.9 0.0 collective-permute-done.1.below_ref
  70.9 0.0 copy-done.2
  70.9 7.4 %electrics.1 = f32[3,8,128,256]{3,2,1,0:T(8,128)} custom-call(f32[3,8,128,256]{3,2,1,0:T(8,128)} %e_hbm.5, f32[3,8,128,256]{3,2,1,0:T(8,128)} %get-tuple-element.28.h_hbm, f32[2,128,256]{2,1,0:T(8,128)S(1)} %collective-permute-done.1.below_ref, f32[8,128,256]{2,1,0:T(8,128)} %sigma_hbm.1, f32[128,128]{1,0:T(8,128)S(1)} %bitcast.15, ...), custom_call_target="tpu_custom_call" | custom-call | bytes 22140000 | tf_op jit(solution)/shard_map/electrics/pallas_call | solution.py:30
Async XLA Ops:
  0.6 18.3 %copy-start.3 = (s32[1,16384]{1,0:T(1,128)S(1)}, s32[1,16384]{1,0:T(1,128)}, u32[]{:S(2)}) copy-start(s32[1,16384]{1,0:T(1,128)} %param.19) | copy-start | bytes 196612
  4.9 17.9 %collective-permute-start = (f32[2,128,256]{2,1,0:T(8,128)}, f32[2,128,256]{2,1,0:T(8,128)S(1)}, u32[]{:S(2)}, u32[]{:S(2)}) collective-permute-start(f32[2,128,256]{2,1,0:T(8,128)} %get-tuple-element.31), channel_id=1, source_target_pairs={{1,0},{2,1},{3,2},{4,3},{5,4},{6,5},{7,6},{8,7},{9,8},{10,9},{11,1... | collective-permute-start | bytes 786440 | tf_op jit(solution)/shard_map/ppermute | solution.py:791
  11.0 17.8 %all-to-all-start = ((f32[128,1,128]{2,1,0:T(1,128)}), f32[128,1,128]{2,1,0:T(1,128)S(1)}, u32[]{:S(2)}, u32[]{:S(2)}) async-start(f32[128,1,128]{2,1,0:T(1,128)} %bitcast.20), calls=%async_computation | async-start | bytes 131072 | tf_op jit(solution)/shard_map/all_to_all | solution.py:800
  22.9 8.1 %copy-start = (f32[32,32,128]{2,1,0:T(8,128)S(1)}, f32[32,32,128]{2,1,0:T(8,128)}, u32[]{:S(2)}) copy-start(f32[32,32,128]{2,1,0:T(8,128)} %a_ref.1) | copy-start | bytes 1572868
  22.9 8.1 %copy-start.4 = (s32[128]{0:T(128)S(1)}, s32[128]{0:T(128)}, u32[]{:S(2)}) copy-start(s32[128]{0:T(128)} %param.20) | copy-start | bytes 1540
  28.7 42.1 %collective-permute-start.1 = (f32[2,128,256]{2,1,0:T(8,128)S(1)}, f32[2,128,256]{2,1,0:T(8,128)S(1)}, u32[]{:S(2)}, u32[]{:S(2)}) collective-permute-start(f32[2,128,256]{2,1,0:T(8,128)S(1)} %get-tuple-element.39), channel_id=1, source_target_pairs={{0,1},{1,2},{2,3},{3,4},{4,5},{5,6},{6,7},{7,8},{8,9},{9,10},{10,1... | collective-permute-start | bytes 786440 | tf_op jit(solution)/shard_map/ppermute | solution.py:791
  31.0 19.8 %copy-start.1 = (f32[32,32,128]{2,1,0:T(8,128)S(1)}, f32[32,32,128]{2,1,0:T(8,128)}, u32[]{:S(2)}) copy-start(f32[32,32,128]{2,1,0:T(8,128)} %b_ref.1) | copy-start | bytes 1572868
  31.0 19.7 %copy-start.5 = (s32[128]{0:T(128)S(1)}, s32[128]{0:T(128)}, u32[]{:S(2)}) copy-start(s32[128]{0:T(128)} %param.21) | copy-start | bytes 1540
  46.1 4.7 %collective-permute-start.2 = (f32[3,32,128]{2,1,0:T(8,128)S(1)}, f32[3,32,128]{2,1,0:T(8,128)S(1)}, u32[]{:S(2)}, u32[]{:S(2)}) collective-permute-start(f32[3,32,128]{2,1,0:T(8,128)S(1)} %get-tuple-element.43), channel_id=1, source_target_pairs={{0,1},{1,2},{2,3},{3,0},{4,5},{5,6},{6,7},{7,4},{8,9},{9,10},{10,1... | collective-permute-start | bytes 147464 | tf_op jit(solution)/shard_map/ppermute | solution.py:796
  51.9 19.0 %all-to-all-start.1 = ((f32[128,1,128]{2,1,0:T(1,128)}), f32[128,1,128]{2,1,0:T(1,128)S(1)}, u32[]{:S(2)}, u32[]{:S(2)}) async-start(f32[128,1,128]{2,1,0:T(1,128)} %bitcast.8), calls=%async_computation.1 | async-start | bytes 131072 | tf_op jit(solution)/shard_map/all_to_all | solution.py:800
  61.0 9.9 %copy-start.2 = (f32[3,1,16384]{2,1,0:T(1,128)S(1)}, f32[3,1,16384]{2,1,0:T(1,128)}, u32[]{:S(2)}) copy-start(f32[3,1,16384]{2,1,0:T(1,128)} %param.18) | copy-start | bytes 589828
